TPU v7x, 32 devices: a whole 2x2x4 slice. The times are simulated.
32 devices in a mesh: dp: 16 (over z, y, x), seq: 2 (over core).
Axes of the slice: x: 2, y: 2, z: 4, core: 2. Of those that a mesh axis runs over, the one named last changes fastest.
Arguments:
- frames: bfloat16 [2, 4096, 768], P(None, ('dp', 'seq')), may hold values from -6 to 6
- clip_lengths: int32 [2, 16, 3], P(None, 'dp'), may hold values from 1 to 192, 256 in all within a row
- conv_weight: bfloat16 [128, 48, 768], P(None, None, 'dp'), may hold values from -0.078125 to 0.078125
- front_gain: bfloat16 [768], P('dp'), may hold values from 0.25 to 1.75
- qkv_weight: bfloat16 [768, 2304], P('dp'), may hold values from -0.3125 to 0.3125
- out_weight: bfloat16 [768, 768], P('dp'), may hold values from -0.875 to 0.875
- middle_gain: bfloat16 [768], P('dp'), may hold values from 0.25 to 1.75
- up_weight: bfloat16 [768, 3072], P('dp'), may hold values from -0.21875 to 0.21875
- down_weight: bfloat16 [3072, 768], P('dp'), may hold values from -0.109375 to 0.109375
- final_gain: bfloat16 [768], P('dp'), may hold values from 0.25 to 1.75
- cotangent: bfloat16 [2, 4096, 768], P(None, ('dp', 'seq')), may hold values from -6 to 6
Outputs:
- output: bfloat16 [2, 4096, 768], P(None, ('dp', 'seq'))
- frames_grad: float32 [2, 4096, 768], P(None, ('dp', 'seq'))
- conv_weight_grad: float32 [128, 48, 768], P(None, None, 'dp')
- front_gain_grad: float32 [768], P('dp')
- qkv_weight_grad: float32 [768, 2304], P('dp')
- out_weight_grad: float32 [768, 768], P('dp')
- middle_gain_grad: float32 [768], P('dp')
- up_weight_grad: float32 [768, 3072], P('dp')
- down_weight_grad: float32 [3072, 768], P('dp')
- final_gain_grad: float32 [768], P('dp')
Inputs may be any that keep to these rules, and one draw needn't show every extreme that they name: `clip_lengths`: the 3 lengths of each pack sum to 256; the longest clip of every pack has exactly 192 frames.
All inputs are finite; a program needn't handle non-finite values.
Results may differ from a plain program's by a relative error of at most 0.019.
Values may be sent and summed in bfloat16 or wider, within the bound.
A program may use at most 176 MiB of HBM per device.

v0:
```python
import jax
import jax.numpy as jnp
from jax import lax
from jax.sharding import PartitionSpec as P

HEAD_DIM = 64
GROUPS = 16
KERNEL = 128


epsilon = 1e-05


def padded_2(array, sides, width):
    for axis, dim in sides:
        size, length = (lax.axis_size(axis), array.shape[dim])
        up = [(i, (i + 1) % size) for i in range(size - 1)]
        down = [(j, i) for i, j in up]
        last = lax.slice_in_dim(array, length - width, length, axis=dim)
        first = lax.slice_in_dim(array, 0, width, axis=dim)
        before = lax.ppermute(last, axis, up)
        after = lax.ppermute(first, axis, down)
        array = jnp.concatenate([before, array, after], axis=dim)
    return array


def norm_forward(values, gain_vector):
    centered = values - jnp.mean(values, axis=-1, keepdims=True)
    inverse = lax.rsqrt(jnp.mean(centered * centered, axis=-1, keepdims=True) + epsilon)
    unit_rows = centered * inverse
    return (unit_rows * gain_vector, unit_rows, inverse)


def norm_backward(grad_out, unit_rows, inverse, gain_vector):
    scaled = grad_out * gain_vector
    inner = jnp.mean(scaled, axis=-1, keepdims=True)
    along = jnp.mean(scaled * unit_rows, axis=-1, keepdims=True)
    return (inverse * (scaled - inner - unit_rows * along), jnp.sum(grad_out * unit_rows, axis=0))


def gelu_slope(values):
    cumulative = 0.5 * (1.0 + lax.erf(values * 0.7071067811865476))
    density = jnp.exp(-0.5 * values * values) * 0.3989422804014327
    return cumulative + values * density


def segment_numbers(lengths, pack_rows):
    ends = jnp.cumsum(lengths)
    position = jnp.arange(pack_rows, dtype=jnp.int32)
    return jnp.sum((position[:, None] >= ends[None, :]).astype(jnp.int32), axis=1)


def conv_forward(padded, kernel):
    result = lax.conv_general_dilated(
        padded[None],
        kernel,
        (1,),
        "VALID",
        dimension_numbers=("NWC", "WIO", "NWC"),
        feature_group_count=GROUPS,
        preferred_element_type=jnp.float32,
    )
    return result[0, : padded.shape[0] - KERNEL]


def conv_input_grad(grad_padded, kernel):
    kernel_taps = kernel.shape[0]
    group_width = kernel.shape[1]
    model_width = kernel.shape[2]
    turned = (
        kernel.reshape(kernel_taps, group_width, GROUPS, group_width)
        .transpose(0, 3, 2, 1)
        .reshape(kernel_taps, group_width, model_width)[::-1]
    )
    result = lax.conv_general_dilated(
        grad_padded[None, 1:],
        turned,
        (1,),
        "VALID",
        dimension_numbers=("NWC", "WIO", "NWC"),
        feature_group_count=GROUPS,
        preferred_element_type=jnp.float32,
    )
    return result[0]


def conv_kernel_grad(padded, grad_conv):
    result = lax.conv_general_dilated(
        padded[:, None, :],
        grad_conv[:, None, :],
        (1,),
        "VALID",
        dimension_numbers=("WCN", "WIO", "WNC"),
        batch_group_count=GROUPS,
        preferred_element_type=jnp.float32,
    )
    return result[:KERNEL]


def masked_scores(query_block, key_heads, query_segments, key_segments):
    scores = jnp.einsum(
        "qhd,khd->hqk", query_block, key_heads, preferred_element_type=jnp.float32
    ) * HEAD_DIM ** (-0.5)
    same_clip = query_segments[:, None] == key_segments[None, :]
    return jnp.where(same_clip[None], scores, -1e30)


def split_heads(heads_in):
    pack_rows = heads_in.shape[0]
    local_heads = heads_in.shape[2] // HEAD_DIM
    split_shape = (pack_rows, local_heads, HEAD_DIM)
    return (
        heads_in[:, 0].reshape(split_shape),
        heads_in[:, 1].reshape(split_shape),
        heads_in[:, 2].reshape(split_shape),
    )


def attend(heads_in, segments):
    pack_rows = heads_in.shape[0]
    part_width = heads_in.shape[2]
    queries, key_heads, value_heads = split_heads(heads_in)
    block_rows = min(512, pack_rows)
    scores = masked_scores(queries, key_heads, segments, segments)
    row_max = jnp.max(scores, axis=-1, keepdims=True)
    shifted = jnp.exp(scores - row_max)
    row_total = jnp.sum(shifted, axis=-1, keepdims=True)
    softmax_probs = (shifted / row_total).astype(jnp.bfloat16)
    pieces = jnp.einsum(
        "hqk,khd->qhd", softmax_probs, value_heads, preferred_element_type=jnp.float32
    ).reshape(block_rows, part_width)
    totals = (row_max + jnp.log(row_total))[:, :, 0]
    return (pieces.astype(jnp.bfloat16), totals)


def attend_back(heads_in, grad_heads, totals, segments):
    pack_rows = heads_in.shape[0]
    part_width = heads_in.shape[2]
    queries, key_heads, value_heads = split_heads(heads_in)
    grad_out = grad_heads.reshape(queries.shape)
    block_rows = min(512, pack_rows)
    scores = masked_scores(queries, key_heads, segments, segments)
    softmax_probs = jnp.exp(scores - totals[:, 0:block_rows, None])
    grad_values = jnp.einsum(
        "hqk,qhd->khd",
        softmax_probs.astype(jnp.bfloat16),
        grad_out,
        preferred_element_type=jnp.float32,
    )
    grad_probs = jnp.einsum(
        "qhd,khd->hqk", grad_out, value_heads, preferred_element_type=jnp.float32
    )
    grad_scores = (
        softmax_probs * (grad_probs - jnp.sum(softmax_probs * grad_probs, axis=-1, keepdims=True))
    ).astype(jnp.bfloat16)
    query_grads = jnp.einsum(
        "hqk,khd->qhd", grad_scores, key_heads, preferred_element_type=jnp.float32
    ).reshape(block_rows, part_width) * HEAD_DIM ** (-0.5)
    grad_keys = jnp.einsum(
        "hqk,qhd->khd", grad_scores, queries, preferred_element_type=jnp.float32
    ) * HEAD_DIM ** (-0.5)
    stacked = jnp.stack(
        [
            query_grads,
            grad_keys.reshape(pack_rows, part_width),
            grad_values.reshape(pack_rows, part_width),
        ],
        axis=1,
    )
    return stacked.astype(jnp.bfloat16)


def micro_step(frames_now, lengths_now, cotangent_now, gathered):
    conv_full, front_full, qkv_full, out_full, middle_full, up_full, down_full, final_full = (
        gathered
    )
    local_rows = frames_now.shape[0]
    model_width = frames_now.shape[1]
    pack_rows = local_rows * lax.axis_size("seq")
    front_vector = front_full.astype(jnp.float32)
    middle_vector = middle_full.astype(jnp.float32)
    final_vector = final_full.astype(jnp.float32)
    segments = segment_numbers(lengths_now, pack_rows)
    padded = padded_2(frames_now, (("seq", 0),), KERNEL // 2)
    convolved = conv_forward(padded, conv_full)
    mixed = frames_now.astype(jnp.float32) + jax.nn.gelu(convolved, approximate=False)
    normed, unit_front, inverse_front = norm_forward(mixed, front_vector)
    normed_low = normed.astype(jnp.bfloat16)
    projected = (
        jnp.dot(normed_low, qkv_full, preferred_element_type=jnp.float32)
        .astype(jnp.bfloat16)
        .reshape(local_rows, 3, model_width)
    )
    heads_in = lax.all_to_all(projected, "seq", split_axis=2, concat_axis=0, tiled=True)
    attended_heads, totals = attend(heads_in, segments)
    attended = lax.all_to_all(attended_heads, "seq", split_axis=0, concat_axis=1, tiled=True)
    branch = jnp.dot(attended, out_full, preferred_element_type=jnp.float32)
    middle, unit_middle, inverse_middle = norm_forward(normed + branch, middle_vector)
    middle_low = middle.astype(jnp.bfloat16)
    hidden = jnp.dot(middle_low, up_full, preferred_element_type=jnp.float32)
    activated = jax.nn.gelu(hidden, approximate=False).astype(jnp.bfloat16)
    feed = jnp.dot(activated, down_full, preferred_element_type=jnp.float32)
    output, unit_final, inverse_final = norm_forward(middle + feed, final_vector)
    grad_final, final_gain_grad = norm_backward(
        cotangent_now.astype(jnp.float32), unit_final, inverse_final, final_vector
    )
    grad_feed = grad_final.astype(jnp.bfloat16)
    down_grad = jnp.einsum("rf,rd->fd", activated, grad_feed, preferred_element_type=jnp.float32)
    grad_hidden = (
        jnp.einsum("rd,fd->rf", grad_feed, down_full, preferred_element_type=jnp.float32)
        * gelu_slope(hidden)
    ).astype(jnp.bfloat16)
    up_grad = jnp.einsum("rd,rf->df", middle_low, grad_hidden, preferred_element_type=jnp.float32)
    grad_middle = grad_final + jnp.einsum(
        "rf,df->rd", grad_hidden, up_full, preferred_element_type=jnp.float32
    )
    grad_mid_in, middle_gain_grad = norm_backward(
        grad_middle, unit_middle, inverse_middle, middle_vector
    )
    grad_branch = grad_mid_in.astype(jnp.bfloat16)
    out_grad = jnp.einsum("re,rd->ed", attended, grad_branch, preferred_element_type=jnp.float32)
    grad_attended = jnp.einsum(
        "rd,ed->re", grad_branch, out_full, preferred_element_type=jnp.float32
    ).astype(jnp.bfloat16)
    grad_heads = lax.all_to_all(grad_attended, "seq", split_axis=1, concat_axis=0, tiled=True)
    grad_heads_qkv = attend_back(heads_in, grad_heads, totals, segments)
    grad_projected = lax.all_to_all(
        grad_heads_qkv, "seq", split_axis=0, concat_axis=2, tiled=True
    ).reshape(local_rows, 3 * model_width)
    qkv_grad = jnp.einsum(
        "rd,re->de", normed_low, grad_projected, preferred_element_type=jnp.float32
    )
    grad_normed = grad_mid_in + jnp.einsum(
        "re,de->rd", grad_projected, qkv_full, preferred_element_type=jnp.float32
    )
    grad_mixed, front_gain_grad = norm_backward(
        grad_normed, unit_front, inverse_front, front_vector
    )
    grad_convolved = (grad_mixed * gelu_slope(convolved)).astype(jnp.bfloat16)
    grad_padded = padded_2(grad_convolved, (("seq", 0),), KERNEL // 2)
    frames_grad = grad_mixed + conv_input_grad(grad_padded, conv_full)
    conv_grad = conv_kernel_grad(padded, grad_convolved)
    weight_grads = (
        conv_grad,
        front_gain_grad,
        qkv_grad,
        out_grad,
        middle_gain_grad,
        up_grad,
        down_grad,
        final_gain_grad,
    )
    return (output.astype(jnp.bfloat16), frames_grad, weight_grads)


def shards(
    frames,
    clip_lengths,
    conv_weight,
    front_gain,
    qkv_weight,
    out_weight,
    middle_gain,
    up_weight,
    down_weight,
    final_gain,
    cotangent,
):
    micro_count = frames.shape[0]
    outputs = []
    frame_grads = []
    running = None
    for micro in range(micro_count):
        current = (
            lax.all_gather(conv_weight, "dp", axis=2, tiled=True),
            lax.all_gather(front_gain, "dp", axis=0, tiled=True),
            lax.all_gather(qkv_weight, "dp", axis=0, tiled=True),
            lax.all_gather(out_weight, "dp", axis=0, tiled=True),
            lax.all_gather(middle_gain, "dp", axis=0, tiled=True),
            lax.all_gather(up_weight, "dp", axis=0, tiled=True),
            lax.all_gather(down_weight, "dp", axis=0, tiled=True),
            lax.all_gather(final_gain, "dp", axis=0, tiled=True),
        )
        output, frame_grad, weight_grads = micro_step(
            frames[micro], clip_lengths[micro, 0], cotangent[micro], current
        )
        outputs.append(output)
        frame_grads.append(frame_grad)
        if micro == 0:
            running = weight_grads
        else:
            running = jax.tree.map(jnp.add, running, weight_grads)
    conv_sum, front_sum, qkv_sum, out_sum, middle_sum, up_sum, down_sum, final_sum = running
    conv_sum, front_sum, qkv_sum, out_sum, middle_sum, up_sum, down_sum, final_sum = (
        lax.psum_scatter(conv_sum, "dp", scatter_dimension=2, tiled=True),
        lax.psum_scatter(front_sum, "dp", scatter_dimension=0, tiled=True),
        lax.psum_scatter(qkv_sum, "dp", scatter_dimension=0, tiled=True),
        lax.psum_scatter(out_sum, "dp", scatter_dimension=0, tiled=True),
        lax.psum_scatter(middle_sum, "dp", scatter_dimension=0, tiled=True),
        lax.psum_scatter(up_sum, "dp", scatter_dimension=0, tiled=True),
        lax.psum_scatter(down_sum, "dp", scatter_dimension=0, tiled=True),
        lax.psum_scatter(final_sum, "dp", scatter_dimension=0, tiled=True),
    )
    conv_sum, front_sum, qkv_sum, out_sum, middle_sum, up_sum, down_sum, final_sum = (
        lax.psum(conv_sum.astype(jnp.bfloat16), "seq").astype(jnp.float32),
        lax.psum(front_sum.astype(jnp.bfloat16), "seq").astype(jnp.float32),
        lax.psum(qkv_sum.astype(jnp.bfloat16), "seq").astype(jnp.float32),
        lax.psum(out_sum.astype(jnp.bfloat16), "seq").astype(jnp.float32),
        lax.psum(middle_sum.astype(jnp.bfloat16), "seq").astype(jnp.float32),
        lax.psum(up_sum.astype(jnp.bfloat16), "seq").astype(jnp.float32),
        lax.psum(down_sum.astype(jnp.bfloat16), "seq").astype(jnp.float32),
        lax.psum(final_sum.astype(jnp.bfloat16), "seq").astype(jnp.float32),
    )
    return (
        jnp.stack(outputs, axis=0),
        jnp.stack(frame_grads, axis=0),
        conv_sum,
        front_sum,
        qkv_sum,
        out_sum,
        middle_sum,
        up_sum,
        down_sum,
        final_sum,
    )


def solution(mesh):
    placed = (
        P(None, ("dp", "seq"), None),
        P(None, "dp", None),
        P(None, None, "dp"),
        P("dp"),
        P("dp", None),
        P("dp", None),
        P("dp"),
        P("dp", None),
        P("dp", None),
        P("dp"),
        P(None, ("dp", "seq"), None),
    )
    return jax.shard_map(
        shards,
        mesh=mesh,
        in_specs=placed,
        out_specs=(
            P(None, ("dp", "seq"), None),
            P(None, ("dp", "seq"), None),
            P(None, None, "dp"),
            P("dp"),
            P("dp", None),
            P("dp", None),
            P("dp"),
            P("dp", None),
            P("dp", None),
            P("dp"),
        ),
        check_vma=False,
    )
```

profile of v0, /device:TPU:0, one launch (start us, length us, event | category | flops | bytes accessed | tf_op | source)
XLA Modules:
  0.0 1720.6 jit_solution(17924273181756926490)
XLA Ops:
  27.2 44.8 %all-reduce.7 = (bf16[768]{0:T(1024)(128)(2,1)S(1)}, bf16[768]{0:T(1024)(128)(2,1)S(1)}, bf16[768]{0:T(1024)(128)(2,1)S(1)}) all-reduce(bf16[768]{0:T(1024)(128)(2,1)S(1)} %dynamic-update-slice, bf16[768]{0:T(1024)(128)(2,1)S(1)} %dynamic-update-slice.1, bf16[768]{0:T(1024)(128)(2,1)S(1)} %dynamic-update-slice.2), channel_id=1, replica_groups=mesh['dp'=16,'seq'=2] {'dp'}, use_global_device_ids=true, to_apply=%add | all-reduce | flops 2304 | bytes 9216
  77.3 61.9 %all-gather.6.cloned.1.call-done = bf16[128,48,768]{0,2,1:T(8,128)(2,1)} async-done(((bf16[128,48,48]{0,2,1:T(8,128)(2,1)}), bf16[128,48,768]{0,2,1:T(8,128)(2,1)}) %all-gather.6.cloned.1.call-update) | async-done | bytes 9437200 | tf_op jit(solution)/shard_map/all_gather | solution.py:275
  139.2 33.9 %copy.227 = bf16[128,48,16,48]{3,1,2,0:T(8,128)(2,1)} copy(bf16[128,48,16,48]{0,3,2,1:T(8,128)(2,1)} %bitcast.314) | data formatting | bytes 18874368 | tf_op jit(solution)/shard_map/all_gather | solution.py:275
  173.1 102.0 %fusion.66 = f32[129,16,48]{2,1,0:T(8,128)} fusion(bf16[128,48,16,48]{3,1,2,0:T(8,128)(2,1)} %copy.227, bf16[1,64,16,48]{3,0,2,1:T(2,128)(2,1)S(1)} %concatenate.63, bf16[1,128,16,48]{3,0,2,1:T(2,128)(2,1)S(1)} %copy.225, bf16[1,64,16,48]{3,0,2,1:T(2,128)(2,1)S(1)} %concatenate.62), kind=kOutput, calls=%fused_computation.123 | convolution fusion | flops 1218576384 | bytes 10226688 | tf_op jit(solution)/shard_map/conv_general_dilated | solution.py:54
  275.2 122.1 %fusion.63 = f32[129,16,48]{2,1,0:T(8,128)} fusion(bf16[128,48,16,48]{3,1,2,0:T(8,128)(2,1)} %copy.227, bf16[1,64,16,48]{3,0,2,1:T(2,128)(2,1)S(1)} %copy-done.72, bf16[1,128,16,48]{3,0,2,1:T(2,128)(2,1)S(1)} %copy-done.66, bf16[1,64,16,48]{3,0,2,1:T(2,128)(2,1)S(1)} %copy-done.73), kind=kOutput, calls=%fused_computation.122 | convolution fusion | flops 1218576384 | bytes 10226688 | tf_op jit(solution)/shard_map/conv_general_dilated | solution.py:54
  421.9 7.7 fusion.27
  474.0 6.7 fusion.336
  497.3 5.0 all_to_all.133
  532.8 4.6 all_to_all.135
  570.2 4.9 convolution_add_fusion.1
  578.1 5.1 convolution_add_fusion.3
  598.7 6.0 fusion.400
  618.1 13.5 copy.262
  631.6 139.1 %rev.6 = bf16[128,48,768]{0,2,1:T(8,128)(2,1)} reverse(bf16[128,48,768]{0,2,1:T(8,128)(2,1)} %bitcast.313), dimensions={0} | reverse | bytes 18874368 | tf_op jit(solution)/shard_map/rev | solution.py:71
  770.7 34.0 %copy.264 = bf16[128,48,16,48]{3,1,2,0:T(8,128)(2,1)} copy(bf16[128,48,16,48]{0,3,2,1:T(8,128)(2,1)} %bitcast.316) | data formatting | bytes 18874368 | tf_op jit(solution)/shard_map/rev | solution.py:71
  807.8 4.7 collective-permute-start.6
  818.2 7.3 convolution_add_fusion.2
  826.8 228.8 %fusion.19 = f32[128,48,16,48]{3,1,2,0:T(8,128)} fusion(bf16[128,1,16,48]{3,1,2,0:T(2,128)(2,1)} %copy.293, bf16[64,1,16,48]{3,1,2,0:T(2,128)(2,1)} %concatenate.69, bf16[128,1,16,48]{3,1,2,0:T(2,128)(2,1)S(1)} %copy-done.65, bf16[64,1,16,48]{3,1,2,0:T(2,128)(2,1)} %concatenate.68), kind=kOutput, calls=%fused_computation.31 | convolution fusion | flops 1209139200 | bytes 19464192 | tf_op jit(solution)/shard_map/slice | solution.py:97
  1055.6 161.2 %convolution_add_fusion = f32[128,48,16,48]{3,1,2,0:T(8,128)} fusion(f32[128,48,16,48]{3,1,2,0:T(8,128)} %fusion.19, bf16[128,1,16,48]{3,1,2,0:T(2,128)(2,1)} %copy.287, bf16[256,1,16,48]{3,1,2,0:T(2,128)(2,1)S(1)} %copy-done.52), kind=kOutput, calls=%fused_computation | convolution fusion | flops 1212678144 | bytes 38338560 | tf_op jit(solution)/shard_map/slice | solution.py:97
  1216.9 39.2 %copy.294 = f32[128,48,16,48]{0,3,2,1:T(8,128)} copy(f32[128,48,16,48]{3,1,2,0:T(8,128)} %convolution_add_fusion) | data formatting | bytes 37748736 | tf_op jit(solution)/shard_map/add | solution.py:292
  1256.2 74.3 %all-reduce.6 = (bf16[768]{0:T(1024)(128)(2,1)S(1)}, bf16[768]{0:T(1024)(128)(2,1)S(1)}, bf16[768]{0:T(1024)(128)(2,1)S(1)}) all-reduce(f32[768]{0:T(1024)S(1)} %add.219, f32[768]{0:T(1024)S(1)} %add.224, f32[768]{0:T(1024)S(1)} %add.227), channel_id=3, replica_groups=mesh['dp'=16,'seq'=2] {'dp'}, use_global_device_ids=true, to_apply=%region_38.39.clone | all-reduce | flops 2304 | bytes 13824
  1345.1 66.0 %fusion.337 = f32[1,128,16,48]{3,0,2,1:T(1,128)} fusion(bf16[1,255,16,48]{3,0,2,1:T(2,128)(2,1)S(1)} %copy.263, bf16[128,48,16,48]{3,1,2,0:T(8,128)(2,1)} %copy.264), kind=kOutput, calls=%fused_computation.515 | convolution fusion | flops 1207959552 | bytes 10222080 | tf_op jit(solution)/shard_map/conv_general_dilated | solution.py:75
  1418.3 197.8 %reduce-scatter.6.cloned.1.call-done = f32[128,48,48]{0,2,1:T(8,128)} async-done(((f32[128,48,768]{0,2,1:T(8,128)}), f32[128,48,48]{0,2,1:T(8,128)}) %reduce-scatter.6.cloned.1.call-update) | async-done | bytes 1179664 | tf_op jit(solution)/shard_map/reduce_scatter | solution.py:295
  1618.2 85.3 %fusion.338 = f32[1,128,16,48]{3,0,2,1:T(1,128)} fusion(bf16[1,255,16,48]{3,0,2,1:T(2,128)(2,1)S(1)} %copy-done.53, bf16[128,48,16,48]{3,1,2,0:T(8,128)(2,1)} %copy.264), kind=kOutput, calls=%fused_computation.516 | convolution fusion | flops 1207959552 | bytes 10222080 | tf_op jit(solution)/shard_map/conv_general_dilated | solution.py:75
  (551 shorter events, 247.1 us)
Async XLA Ops:
  7.2 132.0 %all-gather.6.cloned.1.call-start = ((), (), s32[]{:S(2)}) async-start(), calls=%async_computation.13 | async-start | bytes 10027008 | tf_op jit(solution)/shard_map/all_gather | solution.py:275
  7.9 395.2 %all-gather.8.cloned.1.call-start = ((), (), s32[]{:S(2)}) async-start(), calls=%async_computation.14 | async-start | bytes 3760128 | tf_op jit(solution)/shard_map/all_gather | solution.py:277
  8.7 409.9 %all-gather.10.cloned.1.call-start = ((), (), s32[]{:S(2)}) async-start(), calls=%async_computation.15 | async-start | bytes 1253376 | tf_op jit(solution)/shard_map/all_gather | solution.py:278
  9.4 412.5 %all-gather.12.cloned.1.call-start = ((), (), s32[]{:S(2)}) async-start(), calls=%async_computation.16 | async-start | bytes 5013504 | tf_op jit(solution)/shard_map/all_gather | solution.py:280
  10.0 423.1 %all-gather.14.cloned.1.call-start = ((), (), s32[]{:S(2)}) async-start(), calls=%async_computation.17 | async-start | bytes 5013504 | tf_op jit(solution)/shard_map/all_gather | solution.py:281
  11.1 62.6 %collective-permute-start.1 = (bf16[64,768]{1,0:T(8,128)(2,1)S(1)}, bf16[64,768]{1,0:T(8,128)(2,1)S(1)}, u32[]{:S(2)}, u32[]{:S(2)}) collective-permute-start(bf16[64,768]{1,0:T(8,128)(2,1)S(1)} %get-tuple-element.59), channel_id=1, source_target_pairs={{1,0},{3,2},{5,4},{7,6},{9,8},{11,10},{13,12},{15,14},{17,16},{19,... | collective-permute-start | bytes 294920 | tf_op jit(solution)/shard_map/ppermute | solution.py:22
  12.4 62.0 %collective-permute-start = (bf16[64,768]{1,0:T(8,128)(2,1)S(1)}, bf16[64,768]{1,0:T(8,128)(2,1)S(1)}, u32[]{:S(2)}, u32[]{:S(2)}) collective-permute-start(bf16[64,768]{1,0:T(8,128)(2,1)S(1)} %get-tuple-element.58), channel_id=1, source_target_pairs={{0,1},{2,3},{4,5},{6,7},{8,9},{10,11},{12,13},{14,15},{16,17},{18,... | collective-permute-start | bytes 294920 | tf_op jit(solution)/shard_map/ppermute | solution.py:21
  15.5 59.4 %collective-permute-start.3 = (bf16[64,768]{1,0:T(8,128)(2,1)S(1)}, bf16[64,768]{1,0:T(8,128)(2,1)S(1)}, u32[]{:S(2)}, u32[]{:S(2)}) collective-permute-start(bf16[64,768]{1,0:T(8,128)(2,1)S(1)} %get-tuple-element.60), channel_id=1, source_target_pairs={{1,0},{3,2},{5,4},{7,6},{9,8},{11,10},{13,12},{15,14},{17,16},{19,... | collective-permute-start | bytes 294920 | tf_op jit(solution)/shard_map/ppermute | solution.py:22
  16.8 59.4 %collective-permute-start.2 = (bf16[64,768]{1,0:T(8,128)(2,1)S(1)}, bf16[64,768]{1,0:T(8,128)(2,1)S(1)}, u32[]{:S(2)}, u32[]{:S(2)}) collective-permute-start(bf16[64,768]{1,0:T(8,128)(2,1)S(1)} %get-tuple-element.61), channel_id=1, source_target_pairs={{0,1},{2,3},{4,5},{6,7},{8,9},{10,11},{12,13},{14,15},{16,17},{18,... | collective-permute-start | bytes 294920 | tf_op jit(solution)/shard_map/ppermute | solution.py:21
  173.1 102.1 %copy-start.66 = (bf16[1,128,16,48]{3,0,2,1:T(2,128)(2,1)S(1)}, bf16[1,128,16,48]{3,0,2,1:T(2,128)(2,1)}, u32[]{:S(2)}) copy-start(bf16[1,128,16,48]{3,0,2,1:T(2,128)(2,1)} %copy.239) | copy-start | bytes 589828
  275.2 122.1 %copy-start.64 = (f32[129,16,48]{2,1,0:T(8,128)S(1)}, f32[129,16,48]{2,1,0:T(8,128)}, u32[]{:S(2)}) copy-start(f32[129,16,48]{2,1,0:T(8,128)} %fusion.66) | copy-start | bytes 1188868
  414.8 5.1 all-to-all-start.1
  418.4 992.8 %reduce-scatter.10.cloned.1.call-start = ((), (), s32[]{:S(2)}) async-start(), calls=%async_computation.20 | async-start | bytes 2506752 | tf_op jit(solution)/shard_map/reduce_scatter | solution.py:298
  494.6 918.1 %reduce-scatter.8.cloned.1.call-start = ((), (), s32[]{:S(2)}) async-start(), calls=%async_computation.19 | async-start | bytes 7520256 | tf_op jit(solution)/shard_map/reduce_scatter | solution.py:297
  575.1 839.4 %reduce-scatter.12.cloned.1.call-start = ((), (), s32[]{:S(2)}) async-start(), calls=%async_computation.21 | async-start | bytes 10027008 | tf_op jit(solution)/shard_map/reduce_scatter | solution.py:300
  583.2 833.2 %reduce-scatter.14.cloned.1.call-start = ((), (), s32[]{:S(2)}) async-start(), calls=%async_computation.22 | async-start | bytes 10027008 | tf_op jit(solution)/shard_map/reduce_scatter | solution.py:301
  612.4 724.2 %collective-permute-start.5 = (bf16[64,768]{1,0:T(8,128)(2,1)}, bf16[64,768]{1,0:T(8,128)(2,1)}, u32[]{:S(2)}, u32[]{:S(2)}) collective-permute-start(bf16[64,768]{1,0:T(8,128)(2,1)} %get-tuple-element.65), channel_id=1, source_target_pairs={{1,0},{3,2},{5,4},{7,6},{9,8},{11,10},{13,12},{15,14},{17,16},{19,... | collective-permute-start | bytes 294920 | tf_op jit(solution)/shard_map/ppermute | solution.py:22
  613.6 722.9 %collective-permute-start.4 = (bf16[64,768]{1,0:T(8,128)(2,1)}, bf16[64,768]{1,0:T(8,128)(2,1)}, u32[]{:S(2)}, u32[]{:S(2)}) collective-permute-start(bf16[64,768]{1,0:T(8,128)(2,1)} %get-tuple-element.64), channel_id=1, source_target_pairs={{0,1},{2,3},{4,5},{6,7},{8,9},{10,11},{12,13},{14,15},{16,17},{18,... | collective-permute-start | bytes 294920 | tf_op jit(solution)/shard_map/ppermute | solution.py:21
  806.5 533.4 %collective-permute-start.7 = (bf16[64,768]{1,0:T(8,128)(2,1)}, bf16[64,768]{1,0:T(8,128)(2,1)}, u32[]{:S(2)}, u32[]{:S(2)}) collective-permute-start(bf16[64,768]{1,0:T(8,128)(2,1)} %get-tuple-element.67), channel_id=1, source_target_pairs={{1,0},{3,2},{5,4},{7,6},{9,8},{11,10},{13,12},{15,14},{17,16},{19,... | collective-permute-start | bytes 294920 | tf_op jit(solution)/shard_map/ppermute | solution.py:22
  807.8 532.1 %collective-permute-start.6 = (bf16[64,768]{1,0:T(8,128)(2,1)}, bf16[64,768]{1,0:T(8,128)(2,1)}, u32[]{:S(2)}, u32[]{:S(2)}) collective-permute-start(bf16[64,768]{1,0:T(8,128)(2,1)} %get-tuple-element.66), channel_id=1, source_target_pairs={{0,1},{2,3},{4,5},{6,7},{8,9},{10,11},{12,13},{14,15},{16,17},{18,... | collective-permute-start | bytes 294920 | tf_op jit(solution)/shard_map/ppermute | solution.py:21
  825.6 790.5 %reduce-scatter.6.cloned.1.call-start = ((), (), s32[]{:S(2)}) async-start(), calls=%async_computation.18 | async-start | bytes 20054016 | tf_op jit(solution)/shard_map/reduce_scatter | solution.py:295
  826.8 228.9 %copy-start.52 = (bf16[256,1,16,48]{3,1,2,0:T(2,128)(2,1)S(1)}, bf16[256,1,16,48]{3,1,2,0:T(2,128)(2,1)}, u32[]{:S(2)}) copy-start(bf16[256,1,16,48]{3,1,2,0:T(2,128)(2,1)} %fusion.400) | copy-start | bytes 1179652
  1334.8 373.7 %all-reduce.12.cloned.1.call-start = ((), (), s32[]{:S(2)}) async-start(), calls=%async_computation.23 | async-start | bytes 2949120 | tf_op jit(solution)/shard_map/psum | solution.py:305
  1418.2 200.0 %copy-start.53 = (bf16[1,255,16,48]{3,0,2,1:T(2,128)(2,1)S(1)}, bf16[1,255,16,48]{3,0,2,1:T(2,128)(2,1)}, u32[]{:S(2)}) copy-start(bf16[1,255,16,48]{3,0,2,1:T(2,128)(2,1)} %copy.278) | copy-start | bytes 1175044
  (153 other events, 1818.2 us)
Sparse Core Ops, SparseCore 0:
  10.8 128.4 all-gather.5
  142.0 69.4 all-gather.7
  214.3 54.6 all-gather.9
  271.6 79.3 all-gather.11
  353.6 79.4 all-gather.13
  494.7 126.8 reduce-scatter.9
  627.8 151.1 reduce-scatter.7
  785.6 169.5 reduce-scatter.11
  960.9 170.0 reduce-scatter.13
  1334.9 281.0 reduce-scatter.5
  1620.1 19.7 all-reduce.11
where the time goes:
time: 1750 us; the launch traced here: 1720 us
  matrix products  858 us (49%)
  local copies, waits for them, and re-layouts  356 us (20%)
  waiting for transfers between devices  267 us (15%)
  blocking collectives  153 us (9%)
  other arithmetic  43.9 us (3%)
  starting transfers between devices  24.5 us (1%)
  between operations  17.7 us (1%)
    slice x2, matrix products, conv_kernel_grad(): return result[:KERNEL]  390 us
    conv_general_dilated x2, matrix products, conv_forward(): lax.conv_general_dilated(padded[None], kernel, (1,), 'VALID', dimension_n...  224 us
    reduce_scatter x1, waiting for transfers between devices, shards(): lax.psum_scatter(conv_sum, 'dp', scatter_dimension=2, tiled=True)  198 us
    rev x2, local copies, waits for them, and re-layouts, conv_input_grad(): kernel.reshape(kernel_taps, group_width, GROUPS, group_width)  173 us
    conv_general_dilated x2, matrix products, conv_input_grad(): lax.conv_general_dilated(grad_padded[None, 1:], turned, (1,), 'VALID', di...  151 us
    unnamed x2, blocking collectives  119 us
    all_gather x1, waiting for transfers between devices, shards(): lax.all_gather(conv_weight, 'dp', axis=2, tiled=True)  61.9 us
    add x1, local copies, waits for them, and re-layouts, shards(): running = jax.tree.map(jnp.add, running, weight_grads)  39.2 us
  transfers between devices with their start and end apart: 20, of which 4 were waited for; matrix products, arithmetic and copies ran while one was open for 69% of the time, Pallas kernels for 0%

commit v1 on v0

v1 whole, which is shorter than its diff:
```python
import functools

import jax
import jax.numpy as jnp
from jax import lax
from jax.experimental import pallas as pl
from jax.experimental.pallas import tpu as pltpu
from jax.sharding import PartitionSpec as P

MESH = pl.DeviceIdType.MESH


def dp_factors(size):
    return {16: (4, 2, 2), 128: (4, 4, 8)}.get(size, (size, 1, 1))


def offsets_of(dims):
    return [(i, j, k) for i in range(dims[0]) for j in range(dims[1]) for k in range(dims[2])]


def place(dims, order, position, offsets):
    coords = list(position)
    for axis, offset in zip(order, offsets):
        if offset:
            coords[axis] = lax.rem(coords[axis] + offset, dims[axis])
    return (coords[0] * dims[1] + coords[1]) * dims[2] + coords[2]


def position_of(dims):
    me = lax.axis_index("dp")
    return (me // (dims[1] * dims[2]), lax.rem(me // dims[2], dims[1]), lax.rem(me, dims[2]))


def greet(dims, position, core):
    barrier = pltpu.get_barrier_semaphore()
    count = 1
    pl.semaphore_signal(barrier, inc=1, device_id={"seq": 1 - core}, device_id_type=MESH)
    for axis in range(3):
        for offset in range(1, dims[axis]):
            other = place(dims, (axis,), position, (offset,))
            pl.semaphore_signal(barrier, inc=1, device_id={"dp": other}, device_id_type=MESH)
            count += 1
    pl.semaphore_wait(barrier, count)


ORDERS = ((0, 1, 2), (0, 2, 1))


def gather_kernel(dims, chunks, *refs):
    n_arr = len(refs[:-5]) // 2
    ins, outs = refs[:n_arr], refs[n_arr : 2 * n_arr]
    send_sems, recv_sems, push_send, push_recv, local_sems = refs[2 * n_arr :]
    position = position_of(dims)
    me = lax.axis_index("dp")
    core_index = lax.axis_index("seq")
    greet(dims, position, core_index)
    locals_ = []
    for i in range(n_arr):
        copy = pltpu.make_async_copy(ins[i], outs[i].at[me], local_sems.at[i])
        copy.start()
        locals_.append(copy)

    def run(core):
        order = ORDERS[core]
        sizes = [dims[axis] for axis in order]
        started = []
        counters = [0] * len(chunks)

        def part(which, chunk, side):
            array, rows, lanes = chunks[chunk][side]
            return outs[array].at[which, pl.ds(*rows), pl.ds(*lanes)]

        def own(chunk):
            array, rows, lanes = chunks[chunk][core]
            return ins[array].at[pl.ds(*rows), pl.ds(*lanes)]

        def send(chunk, offsets, level, distance):
            gid = place(dims, order, position, offsets)
            target = place(dims, (order[level],), position, (distance,))
            copy = pltpu.make_async_remote_copy(
                src_ref=own(chunk) if offsets == (0, 0, 0) else part(gid, chunk, core),
                dst_ref=part(gid, chunk, core),
                send_sem=send_sems.at[chunk, counters[chunk]],
                recv_sem=recv_sems.at[chunk, gid],
                device_id={"dp": target},
                device_id_type=MESH,
            )
            counters[chunk] += 1
            copy.start()
            started.append(copy)

        def arrive(chunk, offsets):
            gid = place(dims, order, position, offsets)
            ref = part(gid, chunk, core)
            pltpu.make_async_copy(ref, ref, recv_sems.at[chunk, gid]).wait()

        def push(chunk, offsets):
            gid = place(dims, order, position, offsets)
            ref = part(gid, chunk, core)
            copy = pltpu.make_async_remote_copy(
                src_ref=ref,
                dst_ref=ref,
                send_sem=push_send.at[chunk, gid],
                recv_sem=push_recv.at[chunk, gid],
                device_id={"seq": 1 - core},
                device_id_type=MESH,
            )
            copy.start()
            started.append(copy)

        def spread(chunk, offsets, first):
            for level in range(first, 3):
                for distance in range(1, sizes[level]):
                    send(chunk, offsets, level, distance)

        def stage(chunk, number):
            if number == 0:
                spread(chunk, (0, 0, 0), 0)
            if number == 1:
                for i in range(1, sizes[0]):
                    arrive(chunk, (i, 0, 0))
                    spread(chunk, (i, 0, 0), 1)
                    push(chunk, (i, 0, 0))
            if number == 2:
                for i in range(sizes[0]):
                    for j in range(1, sizes[1]):
                        arrive(chunk, (i, j, 0))
                        spread(chunk, (i, j, 0), 2)
                        push(chunk, (i, j, 0))
            if number == 3:
                for i in range(sizes[0]):
                    for j in range(sizes[1]):
                        for k in range(1, sizes[2]):
                            arrive(chunk, (i, j, k))
                            push(chunk, (i, j, k))

        count = len(chunks)
        for step in range(count + 3):
            for number in range(4):
                if 0 <= step - number < count:
                    stage(step - number, number)
        for chunk in range(count):
            for offsets in offsets_of(dims):
                if offsets != (0, 0, 0):
                    gid = place(dims, (0, 1, 2), position, offsets)
                    ref = part(gid, chunk, 1 - core)
                    pltpu.make_async_copy(ref, ref, push_recv.at[chunk, gid]).wait()
        for copy in started:
            copy.wait_send()

    for core in range(2):
        pl.when(core_index == core)(functools.partial(run, core))
    for copy in locals_:
        copy.wait()


def all_gather(arrays, chunks, dp, collective_id=0):
    dims = dp_factors(dp)
    n = len(chunks)
    any_ = pl.BlockSpec(memory_space=pl.ANY)
    return pl.pallas_call(
        functools.partial(gather_kernel, dims, chunks),
        out_shape=[jax.ShapeDtypeStruct((dp,) + a.shape, a.dtype) for a in arrays],
        in_specs=[any_] * len(arrays),
        out_specs=[any_] * len(arrays),
        scratch_shapes=[
            pltpu.SemaphoreType.DMA((n, dp)),
            pltpu.SemaphoreType.DMA((n, dp)),
            pltpu.SemaphoreType.DMA((n, dp)),
            pltpu.SemaphoreType.DMA((n, dp)),
            pltpu.SemaphoreType.DMA((len(arrays),)),
        ],
        compiler_params=pltpu.CompilerParams(collective_id=collective_id, has_side_effects=True),
    )(*arrays)


def scatter_kernel(dims, chunks, n_arr, *refs):
    ins, outs = refs[:n_arr], refs[n_arr : 2 * n_arr]
    scratch = list(refs[2 * n_arr :])
    n = len(chunks)
    stage_refs, pair_refs = scratch[:n], scratch[n : 2 * n]
    hop_refs = [scratch[(2 + level) * n : (3 + level) * n] for level in range(3)]
    (load_sems, pair_send, pair_recv, hop_send, hop_recv, last_send, last_recv) = scratch[5 * n :]
    position = position_of(dims)
    core_index = lax.axis_index("seq")
    greet(dims, position, core_index)

    def run(core):
        order = ORDERS[core]
        sizes = [dims[axis] for axis in order]
        started = []
        other_order = ORDERS[1 - core]
        other_sizes = [dims[axis] for axis in other_order]

        def part(array_refs, which, chunk, side):
            array, rows, lanes = chunks[chunk][side]
            return array_refs[array].at[which, pl.ds(*rows), pl.ds(*lanes)]

        def slot(level, offsets, distance):
            index = distance - 1
            for i in range(level):
                index = index * sizes[i] + offsets[i]
            return index

        def semaphore(level, index):
            return (1, sizes[0], sizes[0] * sizes[1])[level] + index - 1

        def begin(chunk):
            array = chunks[chunk][core][0]
            theirs = sorted(offsets_of(other_sizes), key=lambda o: (o[2] == 0, o[1] == 0, o[0] == 0))
            mine = sorted(offsets_of(sizes), key=lambda o: (o[2] == 0, o[1] == 0, o[0] == 0))
            for given, kept in zip(theirs, mine):
                gid = place(dims, other_order, position, given)
                copy = pltpu.make_async_remote_copy(
                    src_ref=part(ins, gid, chunk, 1 - core),
                    dst_ref=pair_refs[chunk].at[gid],
                    send_sem=pair_send.at[chunk],
                    recv_sem=pair_recv.at[chunk, gid],
                    device_id={"seq": 1 - core},
                    device_id_type=MESH,
                )
                copy.start()
                gid = place(dims, order, position, kept)
                pltpu.make_async_copy(
                    part(ins, gid, chunk, core), stage_refs[chunk].at[gid], load_sems.at[chunk, gid]
                ).start()

        def combine(chunk, offsets, target):
            gid = place(dims, order, position, offsets)
            own = stage_refs[chunk].at[gid]
            pair = pair_refs[chunk].at[gid]
            pltpu.make_async_copy(own, own, load_sems.at[chunk, gid]).wait()
            pltpu.make_async_copy(pair, pair, pair_recv.at[chunk, gid]).wait()
            terms = [own, pair]
            for level in (2, 1, 0):
                if offsets[level]:
                    break
                for distance in range(1, sizes[level]):
                    index = slot(level, offsets, distance)
                    ref = hop_refs[level][chunk].at[index]
                    pltpu.make_async_copy(ref, ref, hop_recv.at[chunk, semaphore(level, index)]).wait()
                    terms.append(ref)
            height = own.shape[0]

            tall = 16 if height % 16 == 0 else height

            @pl.loop(0, height // tall)
            def _(tile):
                rows = pl.ds(pl.multiple_of(tile * tall, tall), tall)
                total = terms[0][rows, :].astype(jnp.float32)
                for term in terms[1:]:
                    total = total + term[rows, :].astype(jnp.float32)
                if target is None:
                    own[rows, :] = total.astype(own.dtype)
                else:
                    target[rows, :] = total

            return gid

        def send(chunk, offsets):
            level = max(i for i in range(3) if offsets[i])
            gid = combine(chunk, offsets, None)
            index = slot(level, offsets, offsets[level])
            target = place(dims, (order[level],), position, (offsets[level],))
            copy = pltpu.make_async_remote_copy(
                src_ref=stage_refs[chunk].at[gid],
                dst_ref=hop_refs[level][chunk].at[index],
                send_sem=hop_send.at[chunk, semaphore(level, index)],
                recv_sem=hop_recv.at[chunk, semaphore(level, index)],
                device_id={"dp": target},
                device_id_type=MESH,
            )
            copy.start()
            started.append(copy)

        def final(chunk):
            array, rows, lanes = chunks[chunk][core]
            half = outs[array].at[pl.ds(*rows), pl.ds(*lanes)]
            combine(chunk, (0, 0, 0), half)
            copy = pltpu.make_async_remote_copy(
                src_ref=half,
                dst_ref=half,
                send_sem=last_send.at[chunk],
                recv_sem=last_recv.at[chunk],
                device_id={"seq": 1 - core},
                device_id_type=MESH,
            )
            copy.start()
            started.append(copy)

        for chunk in range(n):
            begin(chunk)

        def stage(chunk, number):
            if number == 0:
                for d in range(1, sizes[2]):
                    for i in range(sizes[0]):
                        for j in range(sizes[1]):
                            send(chunk, (i, (j + 1) % sizes[1], d))
            if number == 1:
                for d in range(1, sizes[1]):
                    for i in range(sizes[0]):
                        send(chunk, ((i + 1) % sizes[0], d, 0))
            if number == 2:
                for d in range(1, sizes[0]):
                    send(chunk, (d, 0, 0))
            if number == 3:
                final(chunk)

        for step in range(n + 3):
            for number in range(4):
                if 0 <= step - number < n:
                    stage(step - number, number)
        for chunk in range(n):
            array, rows, lanes = chunks[chunk][1 - core]
            half = outs[array].at[pl.ds(*rows), pl.ds(*lanes)]
            pltpu.make_async_copy(half, half, last_recv.at[chunk]).wait()
            sent = pair_refs[chunk]
            pltpu.make_async_copy(sent, sent, pair_send.at[chunk]).wait()
        for copy in started:
            copy.wait_send()

    for core in range(2):
        pl.when(core_index == core)(functools.partial(run, core))


def hop_slots(dims, core):
    a, b, c = [dims[axis] for axis in ORDERS[core]]
    return (a - 1, a * (b - 1), a * b * (c - 1))


def reduce_scatter(arrays, chunks, dp, collective_id=1):
    dims = dp_factors(dp)
    n = len(chunks)
    any_ = pl.BlockSpec(memory_space=pl.ANY)
    shapes = [(chunk[0][1][1], chunk[0][2][1]) for chunk in chunks]
    slots = [max(pair) for pair in zip(hop_slots(dims, 0), hop_slots(dims, 1))]
    low = jnp.bfloat16
    scratch = [pltpu.VMEM((dp,) + s, low) for s in shapes] * 2
    for level in range(3):
        scratch += [pltpu.VMEM((slots[level],) + s, low) for s in shapes]
    return pl.pallas_call(
        functools.partial(scatter_kernel, dims, chunks, len(arrays)),
        out_shape=[jax.ShapeDtypeStruct(a.shape[1:], jnp.float32) for a in arrays],
        in_specs=[any_] * len(arrays),
        out_specs=[pl.BlockSpec(memory_space=pltpu.VMEM)] * len(arrays),
        scratch_shapes=scratch
        + [
            pltpu.SemaphoreType.DMA((n, dp)),
            pltpu.SemaphoreType.DMA((n,)),
            pltpu.SemaphoreType.DMA((n, dp)),
            pltpu.SemaphoreType.DMA((n, dp)),
            pltpu.SemaphoreType.DMA((n, dp)),
            pltpu.SemaphoreType.DMA((n,)),
            pltpu.SemaphoreType.DMA((n,)),
        ],
        compiler_params=pltpu.CompilerParams(
            collective_id=collective_id, has_side_effects=True, vmem_limit_bytes=58 << 20
        ),
    )(*arrays)


GROUPS = 16
KERNEL = 128
FINE = 16
COARSE = KERNEL // FINE
LANES = 128


def lane_numbers(rows):
    return lax.broadcasted_iota(jnp.int32, (rows, LANES), 1)


def take_group(ref, rows, group, width):
    start = group * width
    base = pl.multiple_of(start // LANES * LANES, LANES)
    window = ref[rows, pl.ds(base, 2 * LANES)]
    turned = pltpu.roll(window, lax.rem(2 * LANES - (start - base), 2 * LANES), 1)[:, :LANES]
    return jnp.where(lane_numbers(turned.shape[0]) < width, turned, 0.0)


def add_group(ref, values, group, width):
    start = group * width
    base = pl.multiple_of(start // LANES * LANES, LANES)
    wide = jnp.concatenate([values, jnp.zeros_like(values)], axis=1)
    ref[:, pl.ds(base, 2 * LANES)] += pltpu.roll(wide, start - base, 1)


def double_96(pair, moved):
    lane = lane_numbers(pair.shape[0])
    turned = pltpu.roll(moved, 96, 1)
    return jnp.where(lane < 96, pair, turned), jnp.where(lane < 64, turned, 0.0)


def double_192(first, second, moved_first, moved_second):
    lane = lane_numbers(first.shape[0])
    a, b = pltpu.roll(moved_first, 64, 1), pltpu.roll(moved_second, 64, 1)
    return first, jnp.where(lane < 64, second, a), jnp.where(lane < 64, a, b)


def fold_lanes(tiles, shift):
    a, b, c = tiles
    lane = lane_numbers(a.shape[0])
    tb, tc = pltpu.roll(b, 64, 1), pltpu.roll(c, 64, 1)
    a, b = shift(a, jnp.where(lane < 64, tb, tc), 4), shift(b, tc, 4)
    lane = lane_numbers(a.shape[0])
    far = jnp.where(lane < 32, pltpu.roll(a, 32, 1), pltpu.roll(b, 32, 1))
    a = shift(a, far, 2)
    a = shift(a, pltpu.roll(a, 80, 1), 1)
    return jnp.where(lane_numbers(a.shape[0]) < 48, a, 0.0)


def forward_kernel(pack, frames, weight, out, patches, padded, total):
    group = pl.program_id(0)
    half = KERNEL // 2
    reach = pack + FINE

    @pl.when(group == 0)
    def _():
        padded[...] = jnp.zeros_like(padded)
        padded[half : half + pack, 0 : frames.shape[1]] = frames[...].astype(jnp.float32)
        total[...] = jnp.zeros_like(total)

    rows = reach + KERNEL - FINE
    one = take_group(padded, slice(0, rows), group, 48)
    lane = lane_numbers(rows - FINE)
    two = one[: rows - FINE] + pltpu.roll(one[FINE:], 48, 1)
    low, high = double_96(two[: rows - 3 * FINE], two[2 * FINE :])
    tiles = double_192(low[:reach], high[:reach], low[4 * FINE :], high[4 * FINE :])
    patch = jnp.concatenate(tiles, axis=1).astype(jnp.bfloat16)
    patches[0] = patch
    product = jnp.dot(patch, weight[0], preferred_element_type=jnp.float32)
    size = pack + 8
    near = product[:size, :384] + product[8 : 8 + size, 384:]

    def shift(base, moved, amount):
        return base + pltpu.roll(moved, size - amount, 0)

    tiles = [near[:, i * LANES : (i + 1) * LANES] for i in range(3)]
    add_group(total, fold_lanes(tiles, shift)[:pack], group, 48)

    @pl.when(group == GROUPS - 1)
    def _():
        out[...] = total[:, : frames.shape[1]]


def conv_forward(frames, weight):
    pack, width = frames.shape
    reach = pack + FINE
    return pl.pallas_call(
        functools.partial(forward_kernel, pack),
        grid=(GROUPS,),
        out_shape=[
            jax.ShapeDtypeStruct((pack, width), jnp.float32),
            jax.ShapeDtypeStruct((GROUPS, reach, 384), jnp.bfloat16),
        ],
        in_specs=[
            pl.BlockSpec((pack, width), lambda g: (0, 0)),
            pl.BlockSpec((1, 384, 768), lambda g: (g, 0, 0)),
        ],
        out_specs=[
            pl.BlockSpec((pack, width), lambda g: (0, 0)),
            pl.BlockSpec((1, reach, 384), lambda g: (g, 0, 0)),
        ],
        scratch_shapes=[
            pltpu.VMEM((pack + KERNEL, width + LANES), jnp.float32),
            pltpu.VMEM((pack, width + LANES), jnp.float32),
        ],
        compiler_params=pltpu.CompilerParams(vmem_limit_bytes=40 << 20),
    )(frames, weight)


def backward_kernel(pack, grads, direct, weight, patches, out, weight_grad, padded, tall, total):
    group = pl.program_id(0)
    reach = pack + FINE
    edge = KERNEL // 2 - FINE

    @pl.when(group == 0)
    def _():
        padded[...] = jnp.zeros_like(padded)
        padded[:pack, : grads.shape[1]] = grads[...].astype(jnp.float32)
        tall[...] = jnp.zeros_like(tall)
        total[...] = jnp.zeros_like(total)
        total[:, : direct.shape[1]] = direct[...]

    def later(values, amount):
        return pltpu.roll(values, amount, 0)

    one = take_group(padded, slice(0, reach), group, 48)
    two = one + pltpu.roll(later(one, 1), 48, 1)
    low, high = double_96(two, later(two, 2))
    tiles = double_192(low, high, later(low, 4), later(high, 4))
    near = jnp.concatenate(tiles, axis=1)
    spread = jnp.concatenate([near, later(near, 8)], axis=1).astype(jnp.bfloat16)
    weight_grad[0] = lax.dot_general(
        patches[0], spread, (((0,), (0,)), ((), ())), preferred_element_type=jnp.float32
    ).astype(jnp.bfloat16)
    tall[edge : edge + reach] = lax.dot_general(
        spread, weight[0], (((1,), (1,)), ((), ())), preferred_element_type=jnp.float32
    )

    def shift(base, moved, amount):
        return base[amount * FINE :] + moved[: base.shape[0] - amount * FINE]

    tiles = [tall[:, i * LANES : (i + 1) * LANES] for i in range(3)]
    add_group(total, fold_lanes(tiles, shift), group, 48)

    @pl.when(group == GROUPS - 1)
    def _():
        out[...] = total[:, : grads.shape[1]]


def conv_backward(grads, direct, weight, patches):
    pack, width = grads.shape
    reach = pack + FINE
    whole = lambda g: (0, 0)
    each = lambda g: (g, 0, 0)
    return pl.pallas_call(
        functools.partial(backward_kernel, pack),
        grid=(GROUPS,),
        out_shape=[
            jax.ShapeDtypeStruct((pack, width), jnp.float32),
            jax.ShapeDtypeStruct(weight.shape, jnp.bfloat16),
        ],
        in_specs=[
            pl.BlockSpec((pack, width), whole),
            pl.BlockSpec((pack, width), whole),
            pl.BlockSpec((1, 384, 768), each),
            pl.BlockSpec((1, reach, 384), each),
        ],
        out_specs=[
            pl.BlockSpec((pack, width), whole),
            pl.BlockSpec((1, 384, 768), each),
        ],
        scratch_shapes=[
            pltpu.VMEM((reach, width + LANES), jnp.float32),
            pltpu.VMEM((pack + KERNEL - FINE, 384), jnp.float32),
            pltpu.VMEM((pack, width + LANES), jnp.float32),
        ],
        compiler_params=pltpu.CompilerParams(vmem_limit_bytes=40 << 20),
    )(grads, direct, weight, patches)


HEAD_DIM = 64
CLIP_EPS = 1e-05
GAIN_ROWS = 16


def norm_forward(values, gain_vector):
    centered = values - jnp.mean(values, axis=-1, keepdims=True)
    inverse = lax.rsqrt(jnp.mean(centered * centered, axis=-1, keepdims=True) + CLIP_EPS)
    unit_rows = centered * inverse
    return (unit_rows * gain_vector, unit_rows, inverse)


def norm_backward(grad_out, unit_rows, inverse, gain_vector):
    scaled = grad_out * gain_vector
    inner = jnp.mean(scaled, axis=-1, keepdims=True)
    along = jnp.mean(scaled * unit_rows, axis=-1, keepdims=True)
    return (inverse * (scaled - inner - unit_rows * along), jnp.sum(grad_out * unit_rows, axis=0))


def gelu_slope(values):
    cumulative = 0.5 * (1.0 + lax.erf(values * 0.7071067811865476))
    density = jnp.exp(-0.5 * values * values) * 0.3989422804014327
    return cumulative + values * density


def segment_numbers(lengths, pack_rows):
    ends = jnp.cumsum(lengths)
    position = jnp.arange(pack_rows, dtype=jnp.int32)
    return jnp.sum((position[:, None] >= ends[None, :]).astype(jnp.int32), axis=1)


def dot(a, b, contract):
    return lax.dot_general(a, b, ((contract[:1], contract[1:]), ((), ())), preferred_element_type=jnp.float32)


def middle_part(frames, convolved, segments, gains, wide, down, cotangent):
    pack, width = frames.shape
    heads = width // HEAD_DIM
    low = jnp.bfloat16
    front_gain, middle_gain, final_gain = gains
    qkv, out_weight, up = wide[:, : 3 * width], wide[:, 3 * width : 4 * width], wide[:, 4 * width :]
    mixed = frames.astype(jnp.float32) + jax.nn.gelu(convolved, approximate=False)
    normed, unit_front, inverse_front = norm_forward(mixed, front_gain)
    normed_low = normed.astype(low)
    projected = dot(normed_low, qkv, (1, 0)).astype(low).reshape(pack, 3, heads, HEAD_DIM)
    queries, keys, values = projected[:, 0], projected[:, 1], projected[:, 2]
    scale = HEAD_DIM ** (-0.5)
    scores = jnp.einsum("qhd,khd->hqk", queries, keys, preferred_element_type=jnp.float32) * scale
    same_clip = segments[:, None] == segments[None, :]
    scores = jnp.where(same_clip[None], scores, -1e30)
    shifted = jnp.exp(scores - jnp.max(scores, axis=-1, keepdims=True))
    probs = shifted / jnp.sum(shifted, axis=-1, keepdims=True)
    probs_low = probs.astype(low)
    attended = (
        jnp.einsum("hqk,khd->qhd", probs_low, values, preferred_element_type=jnp.float32)
        .astype(low)
        .reshape(pack, width)
    )
    branch = dot(attended, out_weight, (1, 0))
    middle, unit_middle, inverse_middle = norm_forward(normed + branch, middle_gain)
    middle_low = middle.astype(low)
    hidden = dot(middle_low, up, (1, 0))
    activated = jax.nn.gelu(hidden, approximate=False).astype(low)
    feed = dot(activated, down, (1, 0))
    output, unit_final, inverse_final = norm_forward(middle + feed, final_gain)
    grad_final, final_gain_grad = norm_backward(
        cotangent.astype(jnp.float32), unit_final, inverse_final, final_gain
    )
    grad_feed = grad_final.astype(low)
    down_grad = dot(activated, grad_feed, (0, 0))
    grad_hidden = (dot(grad_feed, down, (1, 1)) * gelu_slope(hidden)).astype(low)
    up_grad = dot(middle_low, grad_hidden, (0, 0))
    grad_middle = grad_final + dot(grad_hidden, up, (1, 1))
    grad_mid_in, middle_gain_grad = norm_backward(
        grad_middle, unit_middle, inverse_middle, middle_gain
    )
    grad_branch = grad_mid_in.astype(low)
    out_grad = dot(attended, grad_branch, (0, 0))
    grad_attended = dot(grad_branch, out_weight, (1, 1)).astype(low).reshape(pack, heads, HEAD_DIM)
    grad_values = jnp.einsum("hqk,qhd->khd", probs_low, grad_attended, preferred_element_type=jnp.float32)
    grad_probs = jnp.einsum("qhd,khd->hqk", grad_attended, values, preferred_element_type=jnp.float32)
    grad_scores = (
        probs * (grad_probs - jnp.sum(probs * grad_probs, axis=-1, keepdims=True))
    ).astype(low)
    grad_queries = jnp.einsum("hqk,khd->qhd", grad_scores, keys, preferred_element_type=jnp.float32) * scale
    grad_keys = jnp.einsum("hqk,qhd->khd", grad_scores, queries, preferred_element_type=jnp.float32) * scale
    grad_projected = (
        jnp.stack([grad_queries, grad_keys, grad_values], axis=1).astype(low).reshape(pack, 3 * width)
    )
    qkv_grad = dot(normed_low, grad_projected, (0, 0))
    grad_normed = grad_mid_in + dot(grad_projected, qkv, (1, 1))
    grad_mixed, front_gain_grad = norm_backward(grad_normed, unit_front, inverse_front, front_gain)
    grad_convolved = (grad_mixed * gelu_slope(convolved)).astype(low)
    wide_grad = jnp.concatenate([qkv_grad, out_grad, up_grad], axis=1).astype(low)
    gain_grads = jnp.stack([front_gain_grad, middle_gain_grad, final_gain_grad])
    return output.astype(low), grad_mixed, grad_convolved, wide_grad, down_grad.astype(low), gain_grads


def chunks_of(conv_rows, conv_lanes, wide_rows, width, down_rows):
    both = range(2)
    quarter, half = conv_rows // 4, width // 2
    conv = [
        [(0, ((2 * part + core) * quarter, quarter), (0, conv_lanes)) for core in both] for part in both
    ]
    wide = [
        [(1, (0, wide_rows), ((2 * part + core) * 2 * width, 2 * width)) for core in both] for part in both
    ]
    down = [[(2, (0, down_rows), (core * half, half)) for core in both]]
    gain = [[(3, (core * GAIN_ROWS, GAIN_ROWS), (0, LANES)) for core in both]]
    return gain, conv, wide, down


def shards(
    frames,
    clip_lengths,
    conv_weight,
    front_gain,
    qkv_weight,
    out_weight,
    middle_gain,
    up_weight,
    down_weight,
    final_gain,
    cotangent,
):
    dp = lax.axis_size("dp")
    low = jnp.bfloat16
    width = frames.shape[2]
    columns = conv_weight.shape[2]
    group_width = conv_weight.shape[1]
    gain_width = front_gain.shape[0]
    conv_shard = (
        conv_weight.reshape(COARSE, FINE, group_width, columns)
        .transpose(0, 2, 1, 3)
        .reshape(COARSE * group_width, FINE * columns)
    )
    wide_shard = jnp.concatenate([qkv_weight, out_weight, up_weight], axis=1)
    gain_shard = jnp.pad(
        jnp.stack([front_gain, middle_gain, final_gain]),
        ((0, 2 * GAIN_ROWS - 3), (0, LANES - gain_width)),
    )
    parts = (conv_shard, wide_shard, down_weight, gain_shard)
    gain_chunk, conv_chunks, wide_chunks, down_chunk = chunks_of(
        *conv_shard.shape, wide_shard.shape[0], width, down_weight.shape[0]
    )
    conv_all, wide_all, down_all, gain_all = all_gather(
        parts, gain_chunk + conv_chunks + wide_chunks + down_chunk, dp
    )
    split = group_width // columns
    weight = (
        conv_all.reshape(GROUPS, split, COARSE * group_width, FINE, columns)
        .transpose(0, 2, 3, 1, 4)
        .reshape(GROUPS, COARSE * group_width, FINE * group_width)
    )
    wide = wide_all.reshape(width, wide_shard.shape[1])
    down = down_all.reshape(-1, width)
    gains = gain_all[:, :3, :gain_width].transpose(1, 0, 2).reshape(3, width).astype(jnp.float32)

    both = lax.all_to_all(
        jnp.stack([frames, cotangent], axis=1), "seq", split_axis=0, concat_axis=2, tiled=True
    )
    pack_frames, pack_cotangent = both[0, 0], both[0, 1]
    pack = pack_frames.shape[0]
    lengths = lax.dynamic_index_in_dim(clip_lengths[:, 0], lax.axis_index("seq"), 0, False)
    segments = segment_numbers(lengths, pack)

    convolved, patches = conv_forward(pack_frames, weight)
    output, grad_mixed, grad_convolved, wide_grad, down_grad, gain_grads = middle_part(
        pack_frames, convolved, segments, gains, wide, down, pack_cotangent
    )
    frame_grad, conv_grad = conv_backward(grad_convolved, grad_mixed, weight, patches)

    conv_blocks = (
        conv_grad.reshape(GROUPS, COARSE * group_width, FINE, split, columns)
        .transpose(0, 3, 1, 2, 4)
        .reshape((dp,) + conv_shard.shape)
    )
    gain_blocks = jnp.pad(
        gain_grads.astype(low).reshape(3, dp, gain_width).transpose(1, 0, 2),
        ((0, 0), (0, 2 * GAIN_ROWS - 3), (0, LANES - gain_width)),
    )
    conv_sum, wide_sum, down_sum, gain_sum = reduce_scatter(
        (
            conv_blocks,
            wide_grad.reshape((dp,) + wide_shard.shape),
            down_grad.reshape((dp,) + down_weight.shape),
            gain_blocks,
        ),
        gain_chunk + down_chunk + wide_chunks[::-1] + conv_chunks,
        dp,
    )
    conv_sum = (
        conv_sum.reshape(COARSE, group_width, FINE, columns)
        .transpose(0, 2, 1, 3)
        .reshape(conv_weight.shape)
    )
    outputs = lax.all_to_all(output[None], "seq", split_axis=1, concat_axis=0, tiled=True)
    frame_grads = lax.all_to_all(frame_grad[None], "seq", split_axis=1, concat_axis=0, tiled=True)
    return (
        outputs,
        frame_grads,
        conv_sum,
        gain_sum[0, :gain_width],
        wide_sum[:, : 3 * width],
        wide_sum[:, 3 * width : 4 * width],
        gain_sum[1, :gain_width],
        wide_sum[:, 4 * width :],
        down_sum,
        gain_sum[2, :gain_width],
    )


def solution(mesh):
    frames_spec = P(None, ("dp", "seq"), None)
    row, matrix, columns = P("dp"), P("dp", None), P(None, None, "dp")
    return jax.shard_map(
        shards,
        mesh=mesh,
        in_specs=(
            frames_spec,
            P(None, "dp", None),
            columns,
            row,
            matrix,
            matrix,
            row,
            matrix,
            matrix,
            row,
            frames_spec,
        ),
        out_specs=(
            frames_spec,
            frames_spec,
            columns,
            row,
            matrix,
            matrix,
            row,
            matrix,
            matrix,
            row,
        ),
        check_vma=False,
    )
```

time: 1750 us -> 451 us (0.26); the launches traced: 1720 us -> 445 us
  matrix products: 858 us -> 60.1 us
  local copies, waits for them, and re-layouts: 356 us -> 49.8 us
  Pallas kernels: 0 us -> 293 us
  waiting for transfers between devices: 267 us -> 1.92 us
  blocking collectives: 153 us -> 0 us
    slice x2 -> x0, matrix products: 390 us -> none  [conv_kernel_grad(): return result[:KERNEL]]
    conv_general_dilated x4 -> x0, matrix products: 375 us -> none  [the longest x2 224 us: conv_forward(): lax.conv_general_dilated(padded[None], kernel, (1,), 'VALID', dimension_n...]
    pallas_call x0 -> x4, Pallas kernels: none -> 293 us  [the longest x1 136 us: reduce_scatter(): pl.pallas_call(functools.partial(scatter_kernel, dims, chunks, len(arrays...]
    reduce_scatter x5 -> x0, waiting for transfers between devices: 198 us -> none  [the longest x1 198 us: shards(): lax.psum_scatter(conv_sum, 'dp', scatter_dimension=2, tiled=True)]
    rev x2 -> x0, local copies, waits for them, and re-layouts: 173 us -> none  [conv_input_grad(): kernel.reshape(kernel_taps, group_width, GROUPS, group_width)]
    unnamed x2 -> x0, blocking collectives: 119 us -> none
    all_gather x5 -> x0, waiting for transfers between devices: 65.3 us -> none  [the longest x1 61.9 us: shards(): lax.all_gather(conv_weight, 'dp', axis=2, tiled=True)]
    add x1 -> x0, local copies, waits for them, and re-layouts: 39.2 us -> none  [shards(): running = jax.tree.map(jnp.add, running, weight_grads)]
  transfers between devices with their start and end apart: 20 -> 3, of which waited for: 4 -> 1; matrix products, arithmetic and copies ran while one was open for 69% -> 15% of each run, Pallas kernels for 0% -> 36%
where the time goes in v1:
time: 451 us; the launch traced here: 445 us
  Pallas kernels  293 us (65%)
  matrix products  60.1 us (13%)
  local copies, waits for them, and re-layouts  49.8 us (11%)
  other arithmetic  28 us (6%)
  starting transfers between devices  11.4 us (3%)
    pallas_call x1, Pallas kernels, reduce_scatter(): pl.pallas_call(functools.partial(scatter_kernel, dims, chunks, len(arrays...  136 us
    pallas_call x1, Pallas kernels, all_gather(): pl.pallas_call(functools.partial(gather_kernel, dims, chunks), out_shape=...  115 us
    dot_general x12, matrix products, dot(): lax.dot_general(a, b, ((contract[:1], contract[1:]), ((), ())), preferred...  50.3 us
    pallas_call x1, Pallas kernels, conv_backward(): pl.pallas_call(functools.partial(backward_kernel, pack), grid=(GROUPS,),...  24.9 us
    unnamed x98, local copies, waits for them, and re-layouts  23.7 us
    pallas_call x1, Pallas kernels, conv_forward(): pl.pallas_call(functools.partial(forward_kernel, pack), grid=(GROUPS,), o...  16.8 us
  transfers between devices with their start and end apart: 3, of which 1 were waited for; matrix products, arithmetic and copies ran while one was open for 15% of the time, Pallas kernels for 36%

profile of v1, /device:TPU:0, one launch (start us, length us, event | category | flops | bytes accessed | tf_op | source)
XLA Modules:
  0.0 445.4 jit_solution(5761893017468642450)
XLA Ops:
  2.8 3.5 all-to-all-start
  16.2 115.2 %shard_map.186 = (bf16[16,384,768]{2,1,0:T(8,128)(2,1)}, bf16[16,48,6144]{2,1,0:T(8,128)(2,1)}, bf16[16,192,768]{2,1,0:T(8,128)(2,1)}, bf16[16,32,128]{2,1,0:T(8,128)(2,1)}) custom-call(bf16[384,768]{1,0:T(8,128)(2,1)} %reshape.209.refs_0_, bf16[48,6144]{1,0:T(8,128)(2,1)} %pad_maximum_fusion.2.refs_1_, bf16[192,768]{1,0:T(8,128)(2,1)} %refs_2_.1, ...), custom_call_target="tpu_custom_call" | custom-call | tf_op jit(solution)/shard_map/pallas_call | solution.py:161
  131.4 3.7 copy-done.2
  136.1 16.8 %shard_map.187 = (f32[256,768]{1,0:T(8,128)S(1)}, bf16[16,272,384]{2,1,0:T(8,128)(2,1)S(1)}) custom-call(bf16[256,768]{1,0:T(8,128)(2,1)S(1)} %copy-done.5, bf16[16,384,768]{2,1,0:T(8,128)(2,1)S(1)} %copy-done.2), custom_call_target="tpu_custom_call" | custom-call | tf_op jit(solution)/shard_map/pallas_call | solution.py:450
  157.7 4.4 convolution_convert_fusion.3
  164.5 3.4 fusion.65
  168.3 4.1 fusion.86
  177.6 11.2 %fusion.8 = (bf16[256,3072]{1,0:T(8,128)(2,1)S(1)}, f32[256,3072]{1,0:T(8,128)}) fusion(bf16[768,6144]{1,0:T(8,128)(2,1)} %bitcast.158, f32[256,768]{1,0:T(8,128)} %copy-done.12, f32[768]{0:T(1024)S(1)} %mul.251, f32[256]{0:T(256)S(1)} %add_rsqrt_fusion.1, f32[256]{0:T(256)S(1)} %broadcast_multiply_fusion.7), kind=kOutput, calls=%fused_computation.16 | convolution fusion | flops 1259864064 | bytes 10228736 | tf_op jit(solution)/shard_map/dot_general | solution.py:576
  188.8 4.4 fusion.88
  198.2 4.7 %reduce.12 = bf16[256,768]{1,0:T(8,128)(2,1)} reduce(bf16[256,1,768]{2,1,0:T(2,128)(2,1)} %bitcast.145, bf16[]{:T(256)} %broadcast.208), dimensions={1}, to_apply=%bitcast.125.reduce_sub_computation | reduce | bytes 786434
  204.8 4.2 all-to-all-start.1
  209.0 5.7 %fusion.5 = bf16[256,3072]{1,0:T(8,128)(2,1)S(1)} fusion(bf16[3072,768]{1,0:T(8,128)(2,1)} %bitcast.166, f32[256,3072]{1,0:T(8,128)} %get-tuple-element.100, f32[256,768]{1,0:T(8,128)} %copy-done.20, f32[256]{0:T(256)S(1)} %get-tuple-element.106, f32[256]{0:T(256)S(1)} %get-tuple-element.107, f32[768]{0:T(1024)S(1)} %mul.260, f32[256]{0:T(256)S(1)} %add_rsqrt_fusion, ...), kind=kOutput, calls=%fused_computation.12 | convolution fusion | flops 1217593344 | bytes 10624000 | tf_op jit(solution)/shard_map/dot_general | solution.py:576
  214.7 4.8 %multiply_reduce_fusion.1 = (bf16[768]{0:T(1024)(128)(2,1)S(1)}, f32[256]{0:T(256)S(1)}, f32[256]{0:T(256)S(1)}, f32[256,768]{1,0:T(8,128)S(1)}) fusion(f32[256,768]{1,0:T(8,128)S(1)} %copy-done.14, f32[256]{0:T(256)S(1)} %add_rsqrt_fusion.1, f32[256]{0:T(256)S(1)} %broadcast_multiply_fusion.7, f32[768]{0:T(1024)S(1)} %mul.251, ...), kind=kOutput, calls=%fused_computation.84 | convolution fusion | flops 1211300608 | bytes 9059840 | tf_op jit(solution)/shard_map/dot_general | solution.py:576
  225.1 2.9 multiply_reduce_fusion
  232.4 3.9 convolution_convert_fusion
  236.3 3.8 convolution_convert_fusion.1
  240.3 3.6 fusion.29
  252.7 6.6 %pad_maximum_fusion.refs_1_ = bf16[16,48,6144]{2,1,0:T(8,128)(2,1)} fusion(bf16[16,48,3072]{2,1,0:T(8,128)(2,1)} %bitcast.128, bf16[16,48,768]{2,1,0:T(8,128)(2,1)S(1)} %convolution_convert_fusion.4, bf16[16,48,2304]{2,1,0:T(8,128)(2,1)S(1)} %convolution_convert_fusion.2), kind=kLoop, calls=%fused_computation.1 | loop fusion | flops 28311552 | bytes 18874368 | tf_op jit(solution)/shard_map/concatenate | solution.py:637
  259.3 24.9 %shard_map.188 = (f32[256,768]{1,0:T(8,128)S(1)}, bf16[16,384,768]{2,1,0:T(8,128)(2,1)}) custom-call(bf16[256,768]{1,0:T(8,128)(2,1)S(1)} %get-tuple-element.86.grads, f32[256,768]{1,0:T(8,128)S(1)} %get-tuple-element.87.direct, bf16[16,384,768]{2,1,0:T(8,128)(2,1)} %get-tuple-element.22.weight, bf16[16,272,384]{2,1,0:T(8,128)(2,1)S(1)} %get-tuple-element.27.patches), custom_call_target="tpu_custom_call" | custom-call | tf_op jit(solution)/shard_map/pallas_call | solution.py:518
  285.0 135.8 %shard_map.189 = (f32[384,768]{1,0:T(8,128)}, f32[48,6144]{1,0:T(8,128)}, f32[192,768]{1,0:T(8,128)}, f32[32,128]{1,0:T(8,128)}) custom-call(bf16[16,384,768]{2,1,0:T(8,128)(2,1)} %get-tuple-element.29.refs_0_, bf16[16,48,6144]{2,1,0:T(8,128)(2,1)} %pad_maximum_fusion.refs_1_, bf16[16,192,768]{2,1,0:T(8,128)(2,1)} %bitcast.127, bf16[16,32,128]{2,1,0:T(8,128)(2,1)} %pad.9.refs_3_), custom_call_target="tpu_custom_call" | custom-call | tf_op jit(solution)/shard_map/pallas_call | solution.py:342
  426.1 2.6 reshape.218
  428.8 2.6 copy.101
  431.4 3.2 copy.102
  437.6 3.7 all-to-all-start.2
  (158 shorter events, 64.1 us)
Async XLA Ops:
  0.6 167.3 %copy-start = (s32[2,1,3]{2,1,0:T(1,128)S(1)}, s32[2,1,3]{2,1,0:T(1,128)}, u32[]{:S(2)}) copy-start(s32[2,1,3]{2,1,0:T(1,128)} %param.12) | copy-start | bytes 76
  0.7 9.3 %copy-start.37 = (bf16[128,48,48]{0,2,1:T(8,128)(2,1)S(1)}, bf16[128,48,48]{0,2,1:T(8,128)(2,1)}, u32[]{:S(2)}) copy-start(bf16[128,48,48]{0,2,1:T(8,128)(2,1)} %param.13) | copy-start | bytes 1769476
  2.8 5.5 %all-to-all-start = ((bf16[2,2,128,768]{3,2,1,0:T(8,128)(2,1)}), bf16[2,2,128,768]{3,2,1,0:T(8,128)(2,1)S(1)}, u32[]{:S(2)}, u32[]{:S(2)}) async-start(bf16[2,2,128,768]{3,2,1,0:T(8,128)(2,1)} %pad_maximum_fusion.1), calls=%async_computation | async-start | bytes 1572864 | tf_op jit(solution)/shard_map/all_to_all | solution.py:702
  11.0 4.6 %copy-start.42 = (bf16[48]{0:T(256)(128)(2,1)S(1)}, bf16[48]{0:T(256)(128)(2,1)}, u32[]{:S(2)}) copy-start(bf16[48]{0:T(256)(128)(2,1)} %param.20) | copy-start | bytes 292
  11.0 4.6 %copy-start.43 = (bf16[48]{0:T(256)(128)(2,1)S(1)}, bf16[48]{0:T(256)(128)(2,1)}, u32[]{:S(2)}) copy-start(bf16[48]{0:T(256)(128)(2,1)} %param.17) | copy-start | bytes 292
  11.0 4.6 %copy-start.44 = (bf16[48]{0:T(256)(128)(2,1)S(1)}, bf16[48]{0:T(256)(128)(2,1)}, u32[]{:S(2)}) copy-start(bf16[48]{0:T(256)(128)(2,1)} %param.14) | copy-start | bytes 292
  131.4 3.7 copy-start.2
  136.1 17.7 %copy-start.17 = (bf16[1,2,2,128,768]{4,3,2,1,0:T(8,128)(2,1)S(1)}, bf16[1,2,2,128,768]{4,3,2,1,0:T(8,128)(2,1)}, u32[]{:S(2)}) copy-start(bf16[1,2,2,128,768]{4,3,2,1,0:T(8,128)(2,1)} %copy-done.16) | copy-start | bytes 2359300
  177.6 11.3 %copy-start.13 = (f32[256,768]{1,0:T(8,128)S(1)}, f32[256,768]{1,0:T(8,128)}, u32[]{:S(2)}) copy-start(f32[256,768]{1,0:T(8,128)} %copy-done.12) | copy-start | bytes 2359300
  188.8 4.5 copy-start.28
  204.8 232.8 %all-to-all-start.1 = ((bf16[2,2,49152]{2,1,0:T(2,128)(2,1)}), bf16[2,2,49152]{2,1,0:T(2,128)(2,1)}, u32[]{:S(2)}, u32[]{:S(2)}) async-start(bf16[2,2,49152]{2,1,0:T(2,128)(2,1)} %reshape.240), calls=%async_computation.1 | async-start | bytes 786432 | tf_op jit(solution)/shard_map/all_to_all | solution.py:740
  208.9 5.7 %copy-start.14 = (f32[256,768]{1,0:T(8,128)S(1)}, f32[256,768]{1,0:T(8,128)}, u32[]{:S(2)}) copy-start(f32[256,768]{1,0:T(8,128)} %copy-done.12) | copy-start | bytes 2359300
  209.0 5.7 %copy-start.18 = (bf16[1,2,2,128,768]{4,3,2,1,0:T(8,128)(2,1)S(1)}, bf16[1,2,2,128,768]{4,3,2,1,0:T(8,128)(2,1)}, u32[]{:S(2)}) copy-start(bf16[1,2,2,128,768]{4,3,2,1,0:T(8,128)(2,1)} %copy-done.16) | copy-start | bytes 2359300
  209.0 5.7 %copy-start.21 = (f32[256,768]{1,0:T(8,128)S(1)}, f32[256,768]{1,0:T(8,128)}, u32[]{:S(2)}) copy-start(f32[256,768]{1,0:T(8,128)} %copy-done.20) | copy-start | bytes 2359300
  214.7 4.8 %copy-start.34 = (bf16[256,3072]{1,0:T(8,128)(2,1)}, bf16[256,3072]{1,0:T(8,128)(2,1)S(1)}, u32[]{:S(2)}) copy-start(bf16[256,3072]{1,0:T(8,128)(2,1)S(1)} %fusion.5) | copy-start | bytes 4718596
  232.4 3.9 copy-start.15
  232.4 3.9 copy-start.35
  236.3 4.0 copy-start.24
  240.2 3.6 copy-start.26
  240.2 3.6 copy-start.10
  431.4 4.6 %copy-start.7 = (f32[256,768]{1,0:T(8,128)S(1)}, f32[256,768]{1,0:T(8,128)}, u32[]{:S(2)}) copy-start(f32[256,768]{1,0:T(8,128)} %copy-done.6) | copy-start | bytes 2359300
  435.9 9.2 %copy-start.1 = (s32[2,1,3]{2,1,0:T(1,128)S(1)}, s32[2,1,3]{2,1,0:T(1,128)}, u32[]{:S(2)}) copy-start(s32[2,1,3]{2,1,0:T(1,128)} %param.12) | copy-start | bytes 76
  437.6 6.7 %copy-start.36 = (f32[192,768]{1,0:T(8,128)S(1)}, f32[192,768]{1,0:T(8,128)}, u32[]{:S(2)}) copy-start(f32[192,768]{1,0:T(8,128)} %get-tuple-element.126) | copy-start | bytes 1769476
  437.6 5.8 %all-to-all-start.2 = ((f32[1,256,768]{2,0,1:T(1,128)}), f32[1,256,768]{2,0,1:T(1,128)S(1)}, u32[]{:S(2)}, u32[]{:S(2)}) async-start(f32[1,256,768]{2,0,1:T(1,128)} %copy.95), calls=%async_computation.2 | async-start | bytes 1572864 | tf_op jit(solution)/shard_map/all_to_all | solution.py:741
  (24 other events, 42.7 us)

commit v2 on v1

--- a/solution.py
+++ b/solution.py
@@ -46,111 +46,136 @@
 ORDERS = ((0, 1, 2), (0, 2, 1))
 
 
+def by_core(core_index, body):
+    for core in range(2):
+        pl.when(core_index == core)(functools.partial(body, core))
+
+
+class Gather:
+    def __init__(self, dims, chunks, ins, outs, sems):
+        self.dims, self.chunks, self.ins, self.outs = dims, chunks, ins, outs
+        self.send_sems, self.recv_sems, self.push_send, self.push_recv = sems
+        self.position = position_of(dims)
+        self.count = dims[0] * dims[1] * dims[2]
+        self.sent = {}
+
+    def part(self, which, chunk, side):
+        array, rows, lanes = self.chunks[chunk][side]
+        out = self.outs[array]
+        if len(out.shape) == 3:
+            return out.at[which, pl.ds(*rows), pl.ds(*lanes)]
+        first = pl.multiple_of(which * self.ins[array].shape[0] + rows[0], 16)
+        return out.at[pl.ds(first, rows[1]), pl.ds(*lanes)]
+
+    def whole(self, which, array):
+        out, height = self.outs[array], self.ins[array].shape[0]
+        if len(out.shape) == 3:
+            return out.at[which]
+        return out.at[pl.ds(pl.multiple_of(which * height, 16), height)]
+
+    def send(self, core, chunk, offsets, level, distance):
+        order = ORDERS[core]
+        gid = place(self.dims, order, self.position, offsets)
+        array, rows, lanes = self.chunks[chunk][core]
+        mine = self.ins[array].at[pl.ds(*rows), pl.ds(*lanes)]
+        number = self.sent.get((core, chunk), 0)
+        self.sent[core, chunk] = number + 1
+        pltpu.make_async_remote_copy(
+            src_ref=mine if offsets == (0, 0, 0) else self.part(gid, chunk, core),
+            dst_ref=self.part(gid, chunk, core),
+            send_sem=self.send_sems.at[chunk, number],
+            recv_sem=self.recv_sems.at[chunk, gid],
+            device_id={"dp": place(self.dims, (order[level],), self.position, (distance,))},
+            device_id_type=MESH,
+        ).start()
+
+    def spread(self, core, chunk, offsets, first):
+        for level in range(first, 3):
+            for distance in range(1, self.dims[ORDERS[core][level]]):
+                self.send(core, chunk, offsets, level, distance)
+
+    def forward(self, core, chunk, offsets, first):
+        gid = place(self.dims, ORDERS[core], self.position, offsets)
+        ref = self.part(gid, chunk, core)
+        pltpu.make_async_copy(ref, ref, self.recv_sems.at[chunk, gid]).wait()
+        self.spread(core, chunk, offsets, first)
+        pltpu.make_async_remote_copy(
+            src_ref=ref,
+            dst_ref=ref,
+            send_sem=self.push_send.at[chunk, gid],
+            recv_sem=self.push_recv.at[chunk, gid],
+            device_id={"seq": 1 - core},
+            device_id_type=MESH,
+        ).start()
+
+    def tasks(self, core, chunk, stage):
+        sizes = [self.dims[axis] for axis in ORDERS[core]]
+        if stage == 0:
+            return [functools.partial(self.spread, core, chunk, (0, 0, 0), 0)]
+        if stage == 1:
+            places = [(i, 0, 0) for i in range(1, sizes[0])]
+        elif stage == 2:
+            places = [(i, j, 0) for i in range(sizes[0]) for j in range(1, sizes[1])]
+        else:
+            places = [o for o in offsets_of(sizes) if o[2]]
+        return [functools.partial(self.forward, core, chunk, offsets, stage) for offsets in places]
+
+    def steps(self, core, step):
+        done = []
+        for stage in range(4):
+            if 0 <= step - stage < len(self.chunks):
+                done += self.tasks(core, step - stage, stage)
+        return done
+
+    def others(self, body):
+        me = lax.axis_index("dp")
+
+        @pl.loop(1, self.count)
+        def _(offset):
+            body(lax.rem(me + offset, self.count), offset)
+
+    def arrived(self, core, chunk):
+        def body(gid, _):
+            ref = self.part(gid, chunk, 1 - core)
+            pltpu.make_async_copy(ref, ref, self.push_recv.at[chunk, gid]).wait()
+
+        self.others(body)
+
+    def finish(self, core):
+        for chunk in range(len(self.chunks)):
+
+            def body(gid, number, chunk=chunk):
+                ref = self.part(gid, chunk, core)
+                pltpu.make_async_copy(ref, ref, self.push_send.at[chunk, gid]).wait()
+                pltpu.make_async_copy(ref, ref, self.send_sems.at[chunk, number - 1]).wait()
+
+            self.others(body)
+
+
 def gather_kernel(dims, chunks, *refs):
     n_arr = len(refs[:-5]) // 2
     ins, outs = refs[:n_arr], refs[n_arr : 2 * n_arr]
-    send_sems, recv_sems, push_send, push_recv, local_sems = refs[2 * n_arr :]
-    position = position_of(dims)
-    me = lax.axis_index("dp")
+    gather = Gather(dims, chunks, ins, outs, refs[2 * n_arr : 2 * n_arr + 4])
+    local_sems = refs[-1]
     core_index = lax.axis_index("seq")
-    greet(dims, position, core_index)
-    locals_ = []
-    for i in range(n_arr):
-        copy = pltpu.make_async_copy(ins[i], outs[i].at[me], local_sems.at[i])
+    greet(dims, gather.position, core_index)
+    own = [
+        pltpu.make_async_copy(ins[i], outs[i].at[lax.axis_index("dp")], local_sems.at[i])
+        for i in range(n_arr)
+    ]
+    for copy in own:
         copy.start()
-        locals_.append(copy)
 
     def run(core):
-        order = ORDERS[core]
-        sizes = [dims[axis] for axis in order]
-        started = []
-        counters = [0] * len(chunks)
-
-        def part(which, chunk, side):
-            array, rows, lanes = chunks[chunk][side]
-            return outs[array].at[which, pl.ds(*rows), pl.ds(*lanes)]
-
-        def own(chunk):
-            array, rows, lanes = chunks[chunk][core]
-            return ins[array].at[pl.ds(*rows), pl.ds(*lanes)]
-
-        def send(chunk, offsets, level, distance):
-            gid = place(dims, order, position, offsets)
-            target = place(dims, (order[level],), position, (distance,))
-            copy = pltpu.make_async_remote_copy(
-                src_ref=own(chunk) if offsets == (0, 0, 0) else part(gid, chunk, core),
-                dst_ref=part(gid, chunk, core),
-                send_sem=send_sems.at[chunk, counters[chunk]],
-                recv_sem=recv_sems.at[chunk, gid],
-                device_id={"dp": target},
-                device_id_type=MESH,
-            )
-            counters[chunk] += 1
-            copy.start()
-            started.append(copy)
-
-        def arrive(chunk, offsets):
-            gid = place(dims, order, position, offsets)
-            ref = part(gid, chunk, core)
-            pltpu.make_async_copy(ref, ref, recv_sems.at[chunk, gid]).wait()
-
-        def push(chunk, offsets):
-            gid = place(dims, order, position, offsets)
-            ref = part(gid, chunk, core)
-            copy = pltpu.make_async_remote_copy(
-                src_ref=ref,
-                dst_ref=ref,
-                send_sem=push_send.at[chunk, gid],
-                recv_sem=push_recv.at[chunk, gid],
-                device_id={"seq": 1 - core},
-                device_id_type=MESH,
-            )
-            copy.start()
-            started.append(copy)
-
-        def spread(chunk, offsets, first):
-            for level in range(first, 3):
-                for distance in range(1, sizes[level]):
-                    send(chunk, offsets, level, distance)
-
-        def stage(chunk, number):
-            if number == 0:
-                spread(chunk, (0, 0, 0), 0)
-            if number == 1:
-                for i in range(1, sizes[0]):
-                    arrive(chunk, (i, 0, 0))
-                    spread(chunk, (i, 0, 0), 1)
-                    push(chunk, (i, 0, 0))
-            if number == 2:
-                for i in range(sizes[0]):
-                    for j in range(1, sizes[1]):
-                        arrive(chunk, (i, j, 0))
-                        spread(chunk, (i, j, 0), 2)
-                        push(chunk, (i, j, 0))
-            if number == 3:
-                for i in range(sizes[0]):
-                    for j in range(sizes[1]):
-                        for k in range(1, sizes[2]):
-                            arrive(chunk, (i, j, k))
-                            push(chunk, (i, j, k))
-
-        count = len(chunks)
-        for step in range(count + 3):
-            for number in range(4):
-                if 0 <= step - number < count:
-                    stage(step - number, number)
-        for chunk in range(count):
-            for offsets in offsets_of(dims):
-                if offsets != (0, 0, 0):
-                    gid = place(dims, (0, 1, 2), position, offsets)
-                    ref = part(gid, chunk, 1 - core)
-                    pltpu.make_async_copy(ref, ref, push_recv.at[chunk, gid]).wait()
-        for copy in started:
-            copy.wait_send()
-
-    for core in range(2):
-        pl.when(core_index == core)(functools.partial(run, core))
-    for copy in locals_:
+        for step in range(len(chunks) + 3):
+            for task in gather.steps(core, step):
+                task()
+        for chunk in range(len(chunks)):
+            gather.arrived(core, chunk)
+        gather.finish(core)
+
+    by_core(core_index, run)
+    for copy in own:
         copy.wait()
 
 
@@ -410,34 +435,45 @@
     return jnp.where(lane_numbers(a.shape[0]) < 48, a, 0.0)
 
 
+def make_patch(padded, group, pack):
+    reach = pack + FINE
+    one = take_group(padded, slice(0, reach + KERNEL - FINE), group, 48)
+    rows = one.shape[0] - FINE
+    two = one[:rows] + pltpu.roll(one[FINE:], 48, 1)
+    low, high = double_96(two[: rows - 2 * FINE], two[2 * FINE :])
+    tiles = double_192(low[:reach], high[:reach], low[4 * FINE :], high[4 * FINE :])
+    return jnp.concatenate(tiles, axis=1).astype(jnp.bfloat16)
+
+
+def add_forward(total, patch, weight, group, pack):
+    product = jnp.dot(patch, weight, preferred_element_type=jnp.float32)
+    size = pack + 8
+    near = product[:size, :384] + product[8 : 8 + size, 384:]
+
+    def shift(base, moved, amount):
+        return base + pltpu.roll(moved, size - amount, 0)
+
+    tiles = [near[:, i * LANES : (i + 1) * LANES] for i in range(3)]
+    add_group(total, fold_lanes(tiles, shift)[:pack], group, 48)
+
+
+def fill_padded(padded, frames):
+    half = KERNEL // 2
+    padded[...] = jnp.zeros_like(padded)
+    padded[half : half + frames.shape[0], 0 : frames.shape[1]] = frames[...].astype(jnp.float32)
+
+
 def forward_kernel(pack, frames, weight, out, patches, padded, total):
     group = pl.program_id(0)
-    half = KERNEL // 2
-    reach = pack + FINE
 
     @pl.when(group == 0)
     def _():
-        padded[...] = jnp.zeros_like(padded)
-        padded[half : half + pack, 0 : frames.shape[1]] = frames[...].astype(jnp.float32)
+        fill_padded(padded, frames)
         total[...] = jnp.zeros_like(total)
 
-    rows = reach + KERNEL - FINE
-    one = take_group(padded, slice(0, rows), group, 48)
-    lane = lane_numbers(rows - FINE)
-    two = one[: rows - FINE] + pltpu.roll(one[FINE:], 48, 1)
-    low, high = double_96(two[: rows - 3 * FINE], two[2 * FINE :])
-    tiles = double_192(low[:reach], high[:reach], low[4 * FINE :], high[4 * FINE :])
-    patch = jnp.concatenate(tiles, axis=1).astype(jnp.bfloat16)
+    patch = make_patch(padded, group, pack)
     patches[0] = patch
-    product = jnp.dot(patch, weight[0], preferred_element_type=jnp.float32)
-    size = pack + 8
-    near = product[:size, :384] + product[8 : 8 + size, 384:]
-
-    def shift(base, moved, amount):
-        return base + pltpu.roll(moved, size - amount, 0)
-
-    tiles = [near[:, i * LANES : (i + 1) * LANES] for i in range(3)]
-    add_group(total, fold_lanes(tiles, shift)[:pack], group, 48)
+    add_forward(total, patch, weight[0], group, pack)
 
     @pl.when(group == GROUPS - 1)
     def _():
@@ -542,22 +578,19 @@
 
 
 HEAD_DIM = 64
-CLIP_EPS = 1e-05
-GAIN_ROWS = 16
-
-
-def norm_forward(values, gain_vector):
-    centered = values - jnp.mean(values, axis=-1, keepdims=True)
-    inverse = lax.rsqrt(jnp.mean(centered * centered, axis=-1, keepdims=True) + CLIP_EPS)
-    unit_rows = centered * inverse
-    return (unit_rows * gain_vector, unit_rows, inverse)
-
-
-def norm_backward(grad_out, unit_rows, inverse, gain_vector):
-    scaled = grad_out * gain_vector
-    inner = jnp.mean(scaled, axis=-1, keepdims=True)
-    along = jnp.mean(scaled * unit_rows, axis=-1, keepdims=True)
-    return (inverse * (scaled - inner - unit_rows * along), jnp.sum(grad_out * unit_rows, axis=0))
+EPSILON = 1e-05
+ROWS = 32
+TILE = 256
+
+
+def dot(a, b, contract=(1, 0)):
+    return lax.dot_general(
+        a, b, ((contract[:1], contract[1:]), ((), ())), preferred_element_type=jnp.float32
+    )
+
+
+def gelu(values):
+    return values * (0.5 * (1.0 + lax.erf(values * 0.7071067811865476)))
 
 
 def gelu_slope(values):
@@ -566,77 +599,569 @@
     return cumulative + values * density
 
 
-def segment_numbers(lengths, pack_rows):
-    ends = jnp.cumsum(lengths)
-    position = jnp.arange(pack_rows, dtype=jnp.int32)
-    return jnp.sum((position[:, None] >= ends[None, :]).astype(jnp.int32), axis=1)
-
-
-def dot(a, b, contract):
-    return lax.dot_general(a, b, ((contract[:1], contract[1:]), ((), ())), preferred_element_type=jnp.float32)
-
-
-def middle_part(frames, convolved, segments, gains, wide, down, cotangent):
+def unit_norm(values):
+    centered = values - jnp.mean(values, axis=-1, keepdims=True)
+    inverse = lax.rsqrt(jnp.mean(centered * centered, axis=-1, keepdims=True) + EPSILON)
+    return centered * inverse, inverse
+
+
+def norm_back(grad, unit, inverse, gain):
+    scaled = grad * gain
+    inner = jnp.mean(scaled, axis=-1, keepdims=True)
+    along = jnp.mean(scaled * unit, axis=-1, keepdims=True)
+    return inverse * (scaled - inner - unit * along)
+
+
+def row_tiles(pack, body):
+    @pl.loop(0, pack // ROWS)
+    def _(tile):
+        body(pl.ds(pl.multiple_of(tile * ROWS, ROWS), ROWS))
+
+
+def lane_tiles(count, body, first=0):
+    @pl.loop(first, count)
+    def _(tile):
+        body(tile, pl.ds(pl.multiple_of(tile * TILE, TILE), TILE))
+
+
+def clip_mask(lengths, micro, pack):
+    row = lax.broadcasted_iota(jnp.int32, (pack, pack), 0)
+    column = lax.broadcasted_iota(jnp.int32, (pack, pack), 1)
+    row_clip, column_clip = jnp.zeros_like(row), jnp.zeros_like(column)
+    end = 0
+    for clip in range(lengths.shape[1]):
+        end = end + lengths[micro, clip]
+        row_clip += (row >= end).astype(jnp.int32)
+        column_clip += (column >= end).astype(jnp.int32)
+    return row_clip == column_clip
+
+
+def front_norm(frames, convolved, gains, normed, normed_low, unit, inverse):
+    def body(rows):
+        mixed = frames[rows, :].astype(jnp.float32) + gelu(convolved[rows, :])
+        units, inv = unit_norm(mixed)
+        unit[rows, :] = units
+        inverse[rows, :] = jnp.broadcast_to(inv, (ROWS, LANES))
+        total = units * gains[0:1, :]
+        normed[rows, :] = total
+        normed_low[rows, :] = total.astype(normed_low.dtype)
+
+    row_tiles(frames.shape[0], body)
+
+
+def project(normed_low, weight, projected):
+    def body(tile, lanes):
+        projected[:, lanes] = dot(normed_low[...], weight[:, lanes]).astype(projected.dtype)
+
+    lane_tiles(projected.shape[1] // TILE, body)
+
+
+def pair_parts(projected, pair, width):
+    return [
+        projected[:, pl.ds(pl.multiple_of(part * width + pair * LANES, LANES), LANES)] for part in range(3)
+    ]
+
+
+def attend(projected, lengths, micro, probs, attended, first=0, last=None):
+    pack, width = attended.shape
+    low = projected.dtype
+    scale = HEAD_DIM ** (-0.5)
+
+    @pl.loop(first, last or width // LANES)
+    def _(pair):
+        same = clip_mask(lengths, micro, pack)
+        queries, keys, values = pair_parts(projected, pair, width)
+        lane = lax.broadcasted_iota(jnp.int32, (pack, LANES), 1)
+        sides = []
+        for side in range(2):
+            own = (lane < HEAD_DIM) == (side == 0)
+            scores = dot(jnp.where(own, queries, jnp.zeros_like(queries)), keys, (1, 1)) * scale
+            scores = jnp.where(same, scores, -1e30)
+            shifted = jnp.exp(scores - jnp.max(scores, axis=-1, keepdims=True))
+            weights = shifted / jnp.sum(shifted, axis=-1, keepdims=True)
+            probs[2 * pair + side] = weights
+            sides.append(dot(weights.astype(low), values))
+        lanes = pl.ds(pl.multiple_of(pair * LANES, LANES), LANES)
+        attended[:, lanes] = jnp.where(lane < HEAD_DIM, *sides).astype(low)
+
+
+def middle_norm(attended, weight, normed, gains, middle, middle_low, unit, inverse):
+    def body(tile, lanes):
+        middle[:, lanes] = normed[:, lanes] + dot(attended[...], weight[:, lanes])
+
+    lane_tiles(normed.shape[1] // TILE, body)
+
+    def finish(rows):
+        units, inv = unit_norm(middle[rows, :])
+        unit[rows, :] = units
+        inverse[rows, :] = jnp.broadcast_to(inv, (ROWS, LANES))
+        total = units * gains[1:2, :]
+        middle[rows, :] = total
+        middle_low[rows, :] = total.astype(middle_low.dtype)
+
+    row_tiles(normed.shape[0], finish)
+
+
+def feed_up(middle_low, weight, hidden, activated, first=0, last=None):
+    def body(tile, lanes):
+        values = dot(middle_low[...], weight[:, lanes])
+        hidden[:, lanes] = values
+        activated[:, lanes] = gelu(values).astype(activated.dtype)
+
+    lane_tiles(last or hidden.shape[1] // TILE, body, first)
+
+
+def feed_down(activated, weight, middle, gains, cotangent, output, grad_final, gain_grads):
+    def body(tile, lanes):
+        middle[...] += dot(activated[:, lanes], weight[lanes, :])
+
+    lane_tiles(activated.shape[1] // TILE, body)
+    gain_grads[2:3, :] = jnp.zeros((1, middle.shape[1]), jnp.float32)
+
+    def finish(rows):
+        units, inv = unit_norm(middle[rows, :])
+        gain = gains[2:3, :]
+        output[rows, :] = (units * gain).astype(output.dtype)
+        grad = cotangent[rows, :].astype(jnp.float32)
+        gain_grads[2:3, :] += jnp.sum(grad * units, axis=0, keepdims=True)
+        grad_final[rows, :] = norm_back(grad, units, inv, gain)
+
+    row_tiles(middle.shape[0], finish)
+
+
+def feed_back(grad, hidden, activated, middle_low, up, down, up_grad, down_grad):
+    low = activated.dtype
+    grad_feed = grad[...].astype(low)
+    turned = jnp.transpose(middle_low[...].astype(jnp.float32)).astype(low)
+
+    def body(tile, lanes):
+        down_grad[lanes, :] = dot(activated[:, lanes], grad_feed, (0, 0)).astype(low)
+        slope = gelu_slope(hidden[:, lanes])
+        grad_hidden = (dot(grad_feed, down[lanes, :], (1, 1)) * slope).astype(low)
+        up_grad[:, lanes] = dot(turned, grad_hidden).astype(low)
+        grad[...] += dot(grad_hidden, up[:, lanes], (1, 1))
+
+    lane_tiles(hidden.shape[1] // TILE, body)
+
+
+def norm_back_rows(grad, unit, inverse, gains, which, gain_grads):
+    gain_grads[which : which + 1, :] = jnp.zeros((1, grad.shape[1]), jnp.float32)
+
+    def body(rows):
+        incoming, units = grad[rows, :], unit[rows, :]
+        gain_grads[which : which + 1, :] += jnp.sum(incoming * units, axis=0, keepdims=True)
+        grad[rows, :] = norm_back(incoming, units, inverse[rows, 0:1], gains[which : which + 1, :])
+
+    row_tiles(grad.shape[0], body)
+
+
+def branch_back(grad, attended, weight, grad_attended, out_grad):
+    low = attended.dtype
+    grad_branch = grad[...].astype(low)
+
+    def body(tile, lanes):
+        out_grad[lanes, :] = dot(attended[:, lanes], grad_branch, (0, 0)).astype(low)
+        grad_attended[:, lanes] = dot(grad_branch, weight[lanes, :], (1, 1)).astype(low)
+
+    lane_tiles(attended.shape[1] // TILE, body)
+
+
+def attend_back(projected, grad_attended, probs, grad_projected):
+    pack, width = grad_attended.shape
+    low = projected.dtype
+    scale = HEAD_DIM ** (-0.5)
+
+    @pl.loop(0, width // LANES)
+    def _(pair):
+        queries, keys, values = pair_parts(projected, pair, width)
+        grad = grad_attended[:, pl.ds(pl.multiple_of(pair * LANES, LANES), LANES)]
+        lane = lax.broadcasted_iota(jnp.int32, (pack, LANES), 1)
+        sides = []
+        for side in range(2):
+            own = (lane < HEAD_DIM) == (side == 0)
+            weights = probs[2 * pair + side]
+            grad_values = dot(weights.astype(low), grad, (0, 0))
+            grad_probs = dot(jnp.where(own, grad, jnp.zeros_like(grad)), values, (1, 1))
+            along = jnp.sum(weights * grad_probs, axis=-1, keepdims=True)
+            grad_scores = (weights * (grad_probs - along)).astype(low)
+            grad_queries = dot(grad_scores, keys) * scale
+            grad_keys = dot(grad_scores, queries, (0, 0)) * scale
+            sides.append((grad_queries, grad_keys, grad_values))
+        for part in range(3):
+            lanes = pl.ds(pl.multiple_of(part * width + pair * LANES, LANES), LANES)
+            grad_projected[:, lanes] = jnp.where(lane < HEAD_DIM, sides[0][part], sides[1][part]).astype(low)
+
+
+def project_back(grad, grad_projected, unit, gains, weight, qkv_grad):
+    low = grad_projected.dtype
+    turned = jnp.transpose(unit[...] * gains[0:1, :]).astype(low)
+
+    def body(tile, lanes):
+        qkv_grad[:, lanes] = dot(turned, grad_projected[:, lanes]).astype(low)
+        grad[...] += dot(grad_projected[:, lanes], weight[:, lanes], (1, 1))
+
+    lane_tiles(grad_projected.shape[1] // TILE, body)
+
+
+def slope_rows(grad, convolved, grad_convolved):
+    def body(rows):
+        grad_convolved[rows, :] = (grad[rows, :] * gelu_slope(convolved[rows, :])).astype(grad_convolved.dtype)
+
+    row_tiles(grad.shape[0], body)
+
+
+def middle_forward_kernel(
+    lengths, frames, convolved, gains, wide, down, cotangent,
+    output, grad_final, unit_front, inverse_front, projected, probs, attended,
+    unit_middle, inverse_middle, middle_low, hidden, activated, gain_grads,
+    normed, normed_low, middle,
+):
+    width = frames.shape[1]
+    gain_grads[...] = jnp.zeros_like(gain_grads)
+    front_norm(frames, convolved, gains, normed, normed_low, unit_front, inverse_front)
+    project(normed_low, wide.at[:, 0 : 3 * width], projected)
+    attend(projected, lengths, 0, probs, attended)
+    middle_norm(
+        attended, wide.at[:, 3 * width : 4 * width], normed, gains, middle, middle_low, unit_middle,
+        inverse_middle,
+    )
+    feed_up(middle_low, wide.at[:, 4 * width :], hidden, activated)
+    feed_down(activated, down, middle, gains, cotangent, output, grad_final, gain_grads)
+
+
+def middle_backward_kernel(
+    gains, wide, down, convolved, grad_final, unit_front, inverse_front, projected, probs, attended,
+    unit_middle, inverse_middle, middle_low, hidden, activated, last_gain_grad,
+    grad, grad_convolved, wide_grad, down_grad, gain_grads,
+    grad_attended, grad_projected,
+):
+    width = grad.shape[1]
+    gain_grads[...] = last_gain_grad[...]
+    grad[...] = grad_final[...]
+    feed_back(
+        grad, hidden, activated, middle_low, wide.at[:, 4 * width :], down, wide_grad.at[:, 4 * width :],
+        down_grad,
+    )
+    norm_back_rows(grad, unit_middle, inverse_middle, gains, 1, gain_grads)
+    branch_back(
+        grad, attended, wide.at[:, 3 * width : 4 * width], grad_attended,
+        wide_grad.at[:, 3 * width : 4 * width],
+    )
+    attend_back(projected, grad_attended, probs, grad_projected)
+    project_back(
+        grad, grad_projected, unit_front, gains, wide.at[:, 0 : 3 * width], wide_grad.at[:, 0 : 3 * width]
+    )
+    norm_back_rows(grad, unit_front, inverse_front, gains, 0, gain_grads)
+    slope_rows(grad, convolved, grad_convolved)
+
+
+def middle_forward(frames, convolved, lengths, gains, wide, down, cotangent):
     pack, width = frames.shape
+    inner = down.shape[0]
     heads = width // HEAD_DIM
-    low = jnp.bfloat16
-    front_gain, middle_gain, final_gain = gains
-    qkv, out_weight, up = wide[:, : 3 * width], wide[:, 3 * width : 4 * width], wide[:, 4 * width :]
-    mixed = frames.astype(jnp.float32) + jax.nn.gelu(convolved, approximate=False)
-    normed, unit_front, inverse_front = norm_forward(mixed, front_gain)
-    normed_low = normed.astype(low)
-    projected = dot(normed_low, qkv, (1, 0)).astype(low).reshape(pack, 3, heads, HEAD_DIM)
-    queries, keys, values = projected[:, 0], projected[:, 1], projected[:, 2]
-    scale = HEAD_DIM ** (-0.5)
-    scores = jnp.einsum("qhd,khd->hqk", queries, keys, preferred_element_type=jnp.float32) * scale
-    same_clip = segments[:, None] == segments[None, :]
-    scores = jnp.where(same_clip[None], scores, -1e30)
-    shifted = jnp.exp(scores - jnp.max(scores, axis=-1, keepdims=True))
-    probs = shifted / jnp.sum(shifted, axis=-1, keepdims=True)
-    probs_low = probs.astype(low)
-    attended = (
-        jnp.einsum("hqk,khd->qhd", probs_low, values, preferred_element_type=jnp.float32)
-        .astype(low)
-        .reshape(pack, width)
-    )
-    branch = dot(attended, out_weight, (1, 0))
-    middle, unit_middle, inverse_middle = norm_forward(normed + branch, middle_gain)
-    middle_low = middle.astype(low)
-    hidden = dot(middle_low, up, (1, 0))
-    activated = jax.nn.gelu(hidden, approximate=False).astype(low)
-    feed = dot(activated, down, (1, 0))
-    output, unit_final, inverse_final = norm_forward(middle + feed, final_gain)
-    grad_final, final_gain_grad = norm_backward(
-        cotangent.astype(jnp.float32), unit_final, inverse_final, final_gain
-    )
-    grad_feed = grad_final.astype(low)
-    down_grad = dot(activated, grad_feed, (0, 0))
-    grad_hidden = (dot(grad_feed, down, (1, 1)) * gelu_slope(hidden)).astype(low)
-    up_grad = dot(middle_low, grad_hidden, (0, 0))
-    grad_middle = grad_final + dot(grad_hidden, up, (1, 1))
-    grad_mid_in, middle_gain_grad = norm_backward(
-        grad_middle, unit_middle, inverse_middle, middle_gain
-    )
-    grad_branch = grad_mid_in.astype(low)
-    out_grad = dot(attended, grad_branch, (0, 0))
-    grad_attended = dot(grad_branch, out_weight, (1, 1)).astype(low).reshape(pack, heads, HEAD_DIM)
-    grad_values = jnp.einsum("hqk,qhd->khd", probs_low, grad_attended, preferred_element_type=jnp.float32)
-    grad_probs = jnp.einsum("qhd,khd->hqk", grad_attended, values, preferred_element_type=jnp.float32)
-    grad_scores = (
-        probs * (grad_probs - jnp.sum(probs * grad_probs, axis=-1, keepdims=True))
-    ).astype(low)
-    grad_queries = jnp.einsum("hqk,khd->qhd", grad_scores, keys, preferred_element_type=jnp.float32) * scale
-    grad_keys = jnp.einsum("hqk,qhd->khd", grad_scores, queries, preferred_element_type=jnp.float32) * scale
-    grad_projected = (
-        jnp.stack([grad_queries, grad_keys, grad_values], axis=1).astype(low).reshape(pack, 3 * width)
-    )
-    qkv_grad = dot(normed_low, grad_projected, (0, 0))
-    grad_normed = grad_mid_in + dot(grad_projected, qkv, (1, 1))
-    grad_mixed, front_gain_grad = norm_backward(grad_normed, unit_front, inverse_front, front_gain)
-    grad_convolved = (grad_mixed * gelu_slope(convolved)).astype(low)
-    wide_grad = jnp.concatenate([qkv_grad, out_grad, up_grad], axis=1).astype(low)
-    gain_grads = jnp.stack([front_gain_grad, middle_gain_grad, final_gain_grad])
-    return output.astype(low), grad_mixed, grad_convolved, wide_grad, down_grad.astype(low), gain_grads
+    low, full = jnp.bfloat16, jnp.float32
+    shape = jax.ShapeDtypeStruct
+    vmem = pl.BlockSpec(memory_space=pltpu.VMEM)
+    saved = [
+        shape((pack, width), low),
+        shape((pack, width), full),
+        shape((pack, width), full),
+        shape((pack, LANES), full),
+        shape((pack, 3 * width), low),
+        shape((heads, pack, pack), full),
+        shape((pack, width), low),
+        shape((pack, width), full),
+        shape((pack, LANES), full),
+        shape((pack, width), low),
+        shape((pack, inner), full),
+        shape((pack, inner), low),
+        shape((8, width), full),
+    ]
+    return pl.pallas_call(
+        middle_forward_kernel,
+        out_shape=saved,
+        in_specs=[pl.BlockSpec(memory_space=pltpu.SMEM)] + [vmem] * 6,
+        out_specs=[vmem] * len(saved),
+        scratch_shapes=[
+            pltpu.VMEM((pack, width), full),
+            pltpu.VMEM((pack, width), low),
+            pltpu.VMEM((pack, width), full),
+        ],
+        compiler_params=pltpu.CompilerParams(vmem_limit_bytes=58 << 20),
+    )(lengths, frames, convolved, gains, wide, down, cotangent)
+
+
+def middle_backward(gains, wide, down, convolved, kept):
+    pack, width = convolved.shape
+    low, full = jnp.bfloat16, jnp.float32
+    shape = jax.ShapeDtypeStruct
+    vmem = pl.BlockSpec(memory_space=pltpu.VMEM)
+    grads = [
+        shape((pack, width), full),
+        shape((pack, width), low),
+        shape(wide.shape, low),
+        shape(down.shape, low),
+        shape((8, width), full),
+    ]
+    return pl.pallas_call(
+        middle_backward_kernel,
+        out_shape=grads,
+        in_specs=[vmem] * (4 + len(kept)),
+        out_specs=[vmem] * len(grads),
+        scratch_shapes=[pltpu.VMEM((pack, width), low), pltpu.VMEM((pack, 3 * width), low)],
+        compiler_params=pltpu.CompilerParams(vmem_limit_bytes=58 << 20),
+    )(gains, wide, down, convolved, *kept)
+
+
+def weave(tasks, pieces):
+    core_index = lax.axis_index("seq")
+    count, done = len(tasks[0]), 0
+    for number, piece in enumerate(pieces + [None]):
+        until = count if piece is None else (number + 1) * count // (len(pieces) + 1)
+
+        def some(core, first=done, last=until):
+            for task in tasks[core][first:last]:
+                task()
+
+        if until > done:
+            by_core(core_index, some)
+        done = until
+        if piece is not None:
+            piece()
+
+
+def fused_forward_kernel(
+    dims, chunks,
+    lengths, frames, cotangent, conv_shard, wide_shard, down_shard, gain_shard,
+    conv_out, wide_out, down_out, both_output, patches, gains, convolved,
+    grad_final, unit_front, inverse_front, projected, probs, attended, unit_middle, inverse_middle,
+    middle_low, hidden, activated, gain_grads,
+    conv_all, wide_all, down_all, gain_all, pack_frames, pack_cotangent, output, padded, total,
+    gains_wide, normed, normed_low, middle,
+    send_sems, recv_sems, push_send, push_recv, local_sems, pair_sems,
+):
+    ins = (conv_shard, wide_shard, down_shard, gain_shard)
+    outs = (conv_all, wide_all, down_all, gain_all)
+    gather = Gather(dims, chunks, ins, outs, (send_sems, recv_sems, push_send, push_recv))
+    core_index = lax.axis_index("seq")
+    me = lax.axis_index("dp")
+    pack, width = pack_frames.shape
+    half = pack // 2
+    greet(dims, gather.position, core_index)
+
+    here = pl.ds(pl.multiple_of(core_index * half, half), half)
+    there = pl.ds(pl.multiple_of((1 - core_index) * half, half), half)
+
+    def to_partner(source, target, number):
+        return pltpu.make_async_remote_copy(
+            src_ref=source,
+            dst_ref=target,
+            send_sem=pair_sems.at[0, number],
+            recv_sem=pair_sems.at[1, number],
+            device_id={"seq": 1 - core_index},
+            device_id_type=MESH,
+        )
+
+    moves = []
+    for number, (source, target) in enumerate(((frames, pack_frames), (cotangent, pack_cotangent))):
+        moves.append(to_partner(source.at[1 - core_index], target.at[here], number))
+        moves.append(pltpu.make_async_copy(source.at[core_index], target.at[here], local_sems.at[number]))
+    for copy in moves:
+        copy.start()
+    own = [
+        pltpu.make_async_copy(ins[i], gather.whole(me, i), local_sems.at[2 + i]) for i in range(len(ins))
+    ]
+    for copy in own:
+        copy.start()
+
+    def early(core):
+        for chunk in range(3):
+            for task in gather.tasks(core, chunk, 0):
+                task()
+
+    by_core(core_index, early)
+    steps = []
+    for step in range(1, len(chunks) + 3):
+        both = []
+        for core in range(2):
+            tasks = []
+            if 3 <= step + 2 < len(chunks):
+                tasks += gather.tasks(core, step + 2, 0)
+            for stage in (1, 2, 3):
+                if 0 <= step - stage < len(chunks):
+                    tasks += gather.tasks(core, step - stage, stage)
+            both.append(tasks)
+        steps.append(both)
+
+    def gate(*numbers):
+        def body(core):
+            for number in numbers:
+                gather.arrived(core, number)
+
+        by_core(core_index, body)
+
+    for copy in moves[:2]:
+        copy.wait()
+    fill_padded(padded, pack_frames)
+    total[...] = jnp.zeros_like(total)
+
+    def patch_piece(first, last):
+        def piece():
+            @pl.loop(first, last)
+            def _(group):
+                patches[group] = make_patch(padded, group, pack)
+
+        return piece
+
+    def conv_piece(first, last):
+        def piece():
+            @pl.loop(first, last)
+            def _(group):
+                add_forward(total, patches[group], conv_all[group], group, pack)
+
+        return piece
+
+    quarter = GROUPS // 4
+    early_pieces = [patch_piece(i * quarter, (i + 1) * quarter) for i in range(4)]
+    weave(steps[0], early_pieces[:1])
+    weave(steps[1], early_pieces[1:3])
+    weave(steps[2], early_pieces[3:])
+    weave(steps[3], [])
+    weave(steps[4], [])
+    for copy in own:
+        copy.wait()
+    gate(0, 1, 2)
+    saves = [pltpu.make_async_copy(a, b, local_sems.at[6 + i]) for i, (a, b) in enumerate(
+        ((conv_all, conv_out), (wide_all, wide_out), (down_all, down_out)))]
+    saves[0].start()
+    gains_wide[...] = jnp.zeros_like(gains_wide)
+
+    @pl.loop(0, gather.count)
+    def _(shard):
+        add_group(gains_wide, gain_all[shard, 0:16, :].astype(jnp.float32), shard, width // gather.count)
+
+    gains[...] = gains_wide[0:8, 0:width]
+    weave(steps[5], [conv_piece(i, i + 2) for i in range(0, GROUPS, 2)])
+
+    def front_piece():
+        convolved[...] = total[:, :width]
+        front_norm(pack_frames, convolved, gains, normed, normed_low, unit_front, inverse_front)
+
+    def project_piece():
+        gate(3)
+        project(normed_low, wide_all.at[:, 0 : 3 * width], projected)
+
+    def attend_piece(first, last):
+        return lambda: attend(projected, lengths, core_index, probs, attended, first, last)
+
+    def middle_piece():
+        middle_norm(
+            attended, wide_all.at[:, 3 * width : 4 * width], normed, gains, middle, middle_low, unit_middle,
+            inverse_middle,
+        )
+
+    pairs = width // LANES
+    weave(
+        steps[6],
+        [front_piece, project_piece]
+        + [attend_piece(i, i + 2) for i in range(0, pairs, 2)]
+        + [middle_piece],
+    )
+    up = wide_all.at[:, 4 * width :]
+    count = hidden.shape[1] // TILE
+    third = count // 3
+
+    def up_piece(first):
+        def piece():
+            if first == 0:
+                gate(4)
+                saves[1].start()
+            feed_up(middle_low, up, hidden, activated, first, first + third)
+
+        return piece
+
+    weave(steps[7], [up_piece(i) for i in range(0, count, third)])
+    gate(5)
+    saves[2].start()
+    for copy in moves[2:]:
+        copy.wait()
+    gain_grads[...] = jnp.zeros_like(gain_grads)
+    feed_down(activated, down_all, middle, gains, pack_cotangent, output, grad_final, gain_grads)
+    last = to_partner(output.at[there], both_output.at[core_index], 2)
+    last.start()
+    stay = pltpu.make_async_copy(output.at[here], both_output.at[core_index], local_sems.at[9])
+    stay.start()
+    by_core(core_index, gather.finish)
+    for copy in saves + [stay, last]:
+        copy.wait()
+
+
+def fused_forward(frames, cotangent, lengths, shards_in, chunks, dp):
+    dims = dp_factors(dp)
+    n = len(chunks)
+    conv_shard, wide_shard, down_shard, gain_shard = shards_in
+    pack, width = 2 * frames.shape[1], frames.shape[2]
+    inner = down_shard.shape[0] * dp
+    heads = width // HEAD_DIM
+    low, full = jnp.bfloat16, jnp.float32
+    shape = jax.ShapeDtypeStruct
+    vmem = pl.BlockSpec(memory_space=pltpu.VMEM)
+    any_ = pl.BlockSpec(memory_space=pl.ANY)
+    conv_shape = (dp,) + conv_shard.shape
+    wide_shape = (width, wide_shard.shape[1])
+    down_shape = (inner, width)
+    tall = pack + FINE
+    saved = [
+        shape(frames.shape, low),
+        shape((GROUPS, tall, 384), low),
+        shape((8, width), full),
+        shape((pack, width), full),
+        shape((pack, width), full),
+        shape((pack, width), full),
+        shape((pack, LANES), full),
+        shape((pack, 3 * width), low),
+        shape((heads, pack, pack), full),
+        shape((pack, width), low),
+        shape((pack, width), full),
+        shape((pack, LANES), full),
+        shape((pack, width), low),
+        shape((pack, inner), full),
+        shape((pack, inner), low),
+        shape((8, width), full),
+    ]
+    return pl.pallas_call(
+        functools.partial(fused_forward_kernel, dims, chunks),
+        out_shape=[shape(conv_shape, low), shape(wide_shape, low), shape(down_shape, low)] + saved,
+        in_specs=[pl.BlockSpec(memory_space=pltpu.SMEM)] + [any_] * 6,
+        out_specs=[any_] * 3 + [vmem] * len(saved),
+        scratch_shapes=[
+            pltpu.VMEM(conv_shape, low),
+            pltpu.VMEM(wide_shape, low),
+            pltpu.VMEM(down_shape, low),
+            pltpu.VMEM((dp,) + gain_shard.shape, low),
+            pltpu.VMEM((pack, width), low),
+            pltpu.VMEM((pack, width), low),
+            pltpu.VMEM((pack, width), low),
+            pltpu.VMEM((pack + KERNEL, width + LANES), full),
+            pltpu.VMEM((pack, width + LANES), full),
+            pltpu.VMEM((16, width + LANES), full),
+            pltpu.VMEM((pack, width), full),
+            pltpu.VMEM((pack, width), low),
+            pltpu.VMEM((pack, width), full),
+            pltpu.SemaphoreType.DMA((n, dp)),
+            pltpu.SemaphoreType.DMA((n, dp)),
+            pltpu.SemaphoreType.DMA((n, dp)),
+            pltpu.SemaphoreType.DMA((n, dp)),
+            pltpu.SemaphoreType.DMA((10,)),
+            pltpu.SemaphoreType.DMA((2, 3)),
+        ],
+        compiler_params=pltpu.CompilerParams(
+            collective_id=2, has_side_effects=True, vmem_limit_bytes=60 << 20
+        ),
+    )(lengths, frames, cotangent, *shards_in)
+
+
+GAIN_ROWS = 16
 
 
 def chunks_of(conv_rows, conv_lanes, wide_rows, width, down_rows):
@@ -686,30 +1211,36 @@
     gain_chunk, conv_chunks, wide_chunks, down_chunk = chunks_of(
         *conv_shard.shape, wide_shard.shape[0], width, down_weight.shape[0]
     )
-    conv_all, wide_all, down_all, gain_all = all_gather(
-        parts, gain_chunk + conv_chunks + wide_chunks + down_chunk, dp
-    )
+    chunks = gain_chunk + conv_chunks + wide_chunks + down_chunk
     split = group_width // columns
-    weight = (
-        conv_all.reshape(GROUPS, split, COARSE * group_width, FINE, columns)
-        .transpose(0, 2, 3, 1, 4)
-        .reshape(GROUPS, COARSE * group_width, FINE * group_width)
-    )
-    wide = wide_all.reshape(width, wide_shard.shape[1])
-    down = down_all.reshape(-1, width)
-    gains = gain_all[:, :3, :gain_width].transpose(1, 0, 2).reshape(3, width).astype(jnp.float32)
-
-    both = lax.all_to_all(
-        jnp.stack([frames, cotangent], axis=1), "seq", split_axis=0, concat_axis=2, tiled=True
-    )
-    pack_frames, pack_cotangent = both[0, 0], both[0, 1]
-    pack = pack_frames.shape[0]
-    lengths = lax.dynamic_index_in_dim(clip_lengths[:, 0], lax.axis_index("seq"), 0, False)
-    segments = segment_numbers(lengths, pack)
-
-    convolved, patches = conv_forward(pack_frames, weight)
-    output, grad_mixed, grad_convolved, wide_grad, down_grad, gain_grads = middle_part(
-        pack_frames, convolved, segments, gains, wide, down, pack_cotangent
+    if split == 1:
+        (weight, wide, down, outputs, patches, gains, convolved, *kept) = fused_forward(
+            frames, cotangent, clip_lengths[:, 0], parts, chunks, dp
+        )
+    else:
+        conv_all, wide_all, down_all, gain_all = all_gather(parts, chunks, dp)
+        weight = (
+            conv_all.reshape(GROUPS, split, COARSE * group_width, FINE, columns)
+            .transpose(0, 2, 3, 1, 4)
+            .reshape(GROUPS, COARSE * group_width, FINE * group_width)
+        )
+        wide = wide_all.reshape(width, wide_shard.shape[1])
+        down = down_all.reshape(-1, width)
+        gains = gain_all[:, :3, :gain_width].transpose(1, 0, 2).reshape(3, width).astype(jnp.float32)
+        gains = jnp.pad(gains, ((0, 5), (0, 0)))
+        both = lax.all_to_all(
+            jnp.stack([frames, cotangent], axis=1), "seq", split_axis=0, concat_axis=2, tiled=True
+        )
+        pack_frames, pack_cotangent = both[0, 0], both[0, 1]
+        lengths = lax.dynamic_index_in_dim(clip_lengths[:, 0], lax.axis_index("seq"), 0)
+        convolved, patches = conv_forward(pack_frames, weight)
+        output, *kept = middle_forward(
+            pack_frames, convolved, lengths, gains, wide, down, pack_cotangent
+        )
+        outputs = lax.all_to_all(output[None], "seq", split_axis=1, concat_axis=0, tiled=True)
+
+    grad_mixed, grad_convolved, wide_grad, down_grad, gain_grads = middle_backward(
+        gains, wide, down, convolved, kept
     )
     frame_grad, conv_grad = conv_backward(grad_convolved, grad_mixed, weight, patches)
 
@@ -719,7 +1250,7 @@
         .reshape((dp,) + conv_shard.shape)
     )
     gain_blocks = jnp.pad(
-        gain_grads.astype(low).reshape(3, dp, gain_width).transpose(1, 0, 2),
+        gain_grads[:3].astype(low).reshape(3, dp, gain_width).transpose(1, 0, 2),
         ((0, 0), (0, 2 * GAIN_ROWS - 3), (0, LANES - gain_width)),
     )
     conv_sum, wide_sum, down_sum, gain_sum = reduce_scatter(
@@ -737,7 +1268,6 @@
         .transpose(0, 2, 1, 3)
         .reshape(conv_weight.shape)
     )
-    outputs = lax.all_to_all(output[None], "seq", split_axis=1, concat_axis=0, tiled=True)
     frame_grads = lax.all_to_all(frame_grad[None], "seq", split_axis=1, concat_axis=0, tiled=True)
     return (
         outputs,

time: 451 us -> 364 us (0.81); the launches traced: 445 us -> 363 us
  matrix products: 60.1 us -> 0 us
  Pallas kernels: 293 us -> 329 us
  other arithmetic: 28 us -> 1.46 us
  local copies, waits for them, and re-layouts: 49.8 us -> 27.7 us
  starting transfers between devices: 11.4 us -> 4.3 us
    dot_general x18 -> x0, matrix products: 60.1 us -> none  [the longest x12 50.3 us: dot(): lax.dot_general(a, b, ((contract[:1], contract[1:]), ((), ())), preferred...]
    pallas_call x2, Pallas kernels: 132 us -> 163 us  [the longest x1 125 us: fused_forward(): pl.pallas_call(functools.partial(fused_forward_kernel, dims, chunks), out...]
    unnamed x98 -> x29, local copies, waits for them, and re-layouts: 23.7 us -> 10.9 us
    all_to_all x2 -> x0, starting transfers between devices: 7.7 us -> none  [the longest x1 4.17 us: shards(): lax.all_to_all(output[None], 'seq', split_axis=1, concat_axis=0, tiled=True)]
    concatenate x1 -> x0, other arithmetic: 6.59 us -> none  [middle_part(): jnp.concatenate([qkv_grad, out_grad, up_grad], axis=1).astype(low)]
    reduce_sum x7 -> x0, other arithmetic: 5.53 us -> none  [the longest x2 2.87 us: norm_backward(): jnp.sum(grad_out * unit_rows, axis=0)]
    pallas_call x1, Pallas kernels: 136 us -> 141 us  [reduce_scatter(): pl.pallas_call(functools.partial(scatter_kernel, dims, chunks, len(arrays...]
    unnamed x1 -> x0, other arithmetic: 4.69 us -> none
  transfers between devices with their start and end apart: 3 -> 1, of which waited for: 1 -> 0; matrix products, arithmetic and copies ran while one was open for 15% -> 4% of each run, Pallas kernels for 36% -> 39%
where the time goes in v2:
time: 364 us; the launch traced here: 363 us
  Pallas kernels  329 us (90%)
  local copies, waits for them, and re-layouts  27.7 us (8%)
  starting transfers between devices  4.3 us (1%)
    pallas_call x1, Pallas kernels, reduce_scatter(): pl.pallas_call(functools.partial(scatter_kernel, dims, chunks, len(arrays...  141 us
    pallas_call x1, Pallas kernels, fused_forward(): pl.pallas_call(functools.partial(fused_forward_kernel, dims, chunks), out...  125 us
    pallas_call x1, Pallas kernels, middle_backward(): pl.pallas_call(middle_backward_kernel, out_shape=grads, in_specs=[vmem] *...  38.1 us
    pallas_call x1, Pallas kernels, conv_backward(): pl.pallas_call(functools.partial(backward_kernel, pack), grid=(GROUPS,),...  24.8 us
    unnamed x29, local copies, waits for them, and re-layouts  10.9 us
  transfers between devices with their start and end apart: 1, of which 0 were waited for; matrix products, arithmetic and copies ran while one was open for 4% of the time, Pallas kernels for 39%

profile of v2, /device:TPU:0, one launch (start us, length us, event | category | flops | bytes accessed | tf_op | source)
XLA Modules:
  0.0 363.0 jit_solution(4292543687618654972)
XLA Ops:
  0.6 1.8 copy.28
  3.0 2.3 reshape.45.conv_shard
  5.3 0.6 fusion.8.gain_shard
  5.9 0.9 pad_maximum_fusion.wide_shard
  6.7 124.7 %shard_map.186 = (bf16[16,384,768]{2,1,0:T(8,128)(2,1)}, bf16[768,6144]{1,0:T(8,128)(2,1)}, bf16[3072,768]{1,0:T(8,128)(2,1)}, bf16[2,128,768]{2,1,0:T(8,128)(2,...) custom-call(s32[2,3]{1,0:T(2,128)} %bitcast.32, ...), custom_call_target="tpu_custom_call" | custom-call | tf_op jit(solution)/shard_map/pallas_call | solution.py:1132
  131.4 38.1 %shard_map.187 = (f32[256,768]{1,0:T(8,128)}, bf16[256,768]{1,0:T(8,128)(2,1)}, bf16[768,6144]{1,0:T(8,128)(2,1)}, bf16[3072,768]{1,0:T(8,128)(2,1)}, f32[8,768]{1,0:T(8,128)}) custom-call(f32[8,768]{1,0:T(8,128)} %get-tuple-element.41.gains, bf16[768,6144]{1,0:T(8,128)(2,1)} %get-tuple-element.42.wide, bf16[3072,768]{1,0:T(8,128)(2,1)} %get-tuple-element.43.down, ...), custom_call_target="tpu_custom_call" | custom-call | tf_op jit(solution)/shard_map/pallas_call | solution.py:906
  169.5 1.1 copy-done.1
  170.7 1.0 copy-done.2
  171.7 24.8 %shard_map.188 = (f32[256,768]{1,0:T(8,128)S(1)}, bf16[16,384,768]{2,1,0:T(8,128)(2,1)}) custom-call(bf16[256,768]{1,0:T(8,128)(2,1)S(1)} %copy-done.2, f32[256,768]{1,0:T(8,128)S(1)} %copy-done.1, bf16[16,384,768]{2,1,0:T(8,128)(2,1)} %get-tuple-element.59.weight, bf16[16,272,384]{2,1,0:T(8,128)(2,1)S(1)} %copy-done), custom_call_target="tpu_custom_call" | custom-call | tf_op jit(solution)/shard_map/pallas_call | solution.py:554
  196.5 1.7 copy.30
  198.2 4.3 %all-to-all-start = ((f32[1,256,768]{2,0,1:T(1,128)}), f32[1,256,768]{2,0,1:T(1,128)}, u32[]{:S(2)}, u32[]{:S(2)}) async-start(f32[1,256,768]{2,0,1:T(1,128)} %copy.30), calls=%async_computation | async-start | bytes 1572864 | tf_op jit(solution)/shard_map/all_to_all | solution.py:1271
  202.5 0.7 slice.34
  203.3 0.7 pad.9.refs_3_
  204.0 141.2 %shard_map.189 = (f32[384,768]{1,0:T(8,128)}, f32[48,6144]{1,0:T(8,128)}, f32[192,768]{1,0:T(8,128)}, f32[32,128]{1,0:T(8,128)}) custom-call(bf16[16,384,768]{2,1,0:T(8,128)(2,1)} %get-tuple-element.62.refs_0_, bf16[16,48,6144]{2,1,0:T(8,128)(2,1)} %bitcast.27, bf16[16,192,768]{2,1,0:T(8,128)(2,1)} %bitcast.29, bf16[16,32,128]{2,1,0:T(8,128)(2,1)} %pad.9.refs_3_), custom_call_target="tpu_custom_call" | custom-call | tf_op jit(solution)/shard_map/pallas_call | solution.py:367
  345.2 1.7 slice.25
  346.9 1.8 slice.24
  348.7 0.9 slice.27
  349.5 1.3 slice_bitcast_fusion
  350.8 2.6 reshape.49
  353.5 2.6 copy.32
  356.1 3.2 copy.33
  359.3 2.1 copy.34
  361.4 0.7 copy.39
  362.2 0.8 copy.40
  (26 shorter events, 0.6 us)
Async XLA Ops:
  2.9 2.3 copy-start.9
  2.9 2.3 copy-start.10
  2.9 2.3 copy-start.11
  2.9 2.9 copy-start.6
  3.0 2.9 copy-start.7
  3.0 2.9 copy-start.8
  131.4 38.1 %copy-start = (bf16[16,272,384]{2,1,0:T(8,128)(2,1)S(1)}, bf16[16,272,384]{2,1,0:T(8,128)(2,1)}, u32[]{:S(2)}) copy-start(bf16[16,272,384]{2,1,0:T(8,128)(2,1)} %get-tuple-element.60.patches) | copy-start | bytes 10027012
  169.5 1.1 copy-start.1
  170.7 1.0 copy-start.2
  198.2 161.1 %all-to-all-start = ((f32[1,256,768]{2,0,1:T(1,128)}), f32[1,256,768]{2,0,1:T(1,128)}, u32[]{:S(2)}, u32[]{:S(2)}) async-start(f32[1,256,768]{2,0,1:T(1,128)} %copy.30), calls=%async_computation | async-start | bytes 1572864 | tf_op jit(solution)/shard_map/all_to_all | solution.py:1271
  345.2 3.5 copy-start.3
  359.3 2.2 copy-start.5
  359.3 2.9 copy-start.4
